TPU v7x, 128 devices: a whole 4x4x4 slice. The times are simulated.
128 devices in a mesh: grp: 16 (over y, z), mem: 8 (over x, core).
Axes of the slice: x: 4, y: 4, z: 4, core: 2. Of those that a mesh axis runs over, the one named last changes fastest.
Arguments:
- embeds: bfloat16 [65536, 768], P(('grp', 'mem')), may hold values from -200 to 200
- cluster: int32 [65536], P(('grp', 'mem')), may hold values from 0 to 199
- dest: int32 [65536], P(('grp', 'mem')), may hold values from 0 to 1023, as said below
Outputs:
- best: float32 [65536], P(('grp', 'mem'))
Inputs may be any that keep to these rules, and one draw needn't show every extreme that they name: The embeddings of one device name distinct slots; slot s belongs to device s // 8 of grp+mem (grp slowest). All embeddings of one cluster belong to devices of one grp index, that is one value of dest // 64. Each grp index has one spread cluster: exactly the slots with s % 8 < 2 hold it, on any member. Every other cluster's embeddings all go to slots of one device. In every draw some device has all 8 of its slots filled by every device.
All inputs are finite; a program needn't handle non-finite values.
Results may differ from a plain program's by a relative error of at most 0.00054.
Values may be sent and summed in bfloat16 or wider, within the bound.
No kernel may reach another device: no remote copies, remote signals or barrier semaphores. Data moves between devices by JAX's collectives and lax.ppermute only.
A program may use at most 64 MiB of HBM per device.

v0:
```python
import jax
import jax.numpy as jnp
from jax import lax
from jax.sharding import PartitionSpec as P


def fold_with(queries, query_labels, query_index, current, pieces):
    columns, column_labels = pieces
    scores = lax.dot_general(
        queries, columns, (((1,), (1,)), ((), ())), preferred_element_type=jnp.float32
    )
    index = jnp.arange(columns.shape[0], dtype=jnp.int32)
    same = (query_labels[:, None] == column_labels[None, :]) & (
        query_index[:, None] != index[None, :]
    )
    return jnp.maximum(current, jnp.max(jnp.where(same, scores, jnp.float32(-1.0)), axis=1))


def shards(embeds, cluster, dest):
    values = embeds.astype(jnp.float32)
    unit = (values * lax.rsqrt(jnp.sum(values * values, axis=1, keepdims=True) + 1e-06)).astype(
        jnp.bfloat16
    )
    n_grp = lax.axis_size("grp")
    n_mem = lax.axis_size("mem")
    devices = n_grp * n_mem
    row_count = embeds.shape[0]
    width = embeds.shape[1]
    capacity = max(2, (2 * row_count + devices - 1) // devices)
    slots = devices * capacity
    labels = cluster.astype(jnp.float32).astype(jnp.bfloat16)
    outgoing = jnp.zeros((slots, width), jnp.bfloat16).at[dest].set(unit)
    out_labels = jnp.full((slots,), -1.0, jnp.bfloat16).at[dest].set(labels)
    initial = jnp.full((slots,), -1.0, jnp.float32)
    own = lax.axis_index("mem") * slots + jnp.arange(slots, dtype=jnp.int32)
    arrived, arrived_labels = (
        lax.all_to_all(
            outgoing.reshape(devices, capacity, width),
            ("grp", "mem"),
            split_axis=0,
            concat_axis=0,
            tiled=True,
        ),
        lax.all_to_all(
            out_labels.reshape(devices, capacity),
            ("grp", "mem"),
            split_axis=0,
            concat_axis=0,
            tiled=True,
        ),
    )
    local = arrived.reshape(slots, width)
    local_labels = arrived_labels.reshape(slots)
    results = fold_with(
        local,
        local_labels,
        own,
        initial,
        (
            lax.all_gather(local, "mem", axis=0, tiled=True),
            lax.all_gather(local_labels, "mem", axis=0, tiled=True),
        ),
    )
    returned = lax.all_to_all(
        results.reshape(devices, capacity), ("grp", "mem"), split_axis=0, concat_axis=0, tiled=True
    )
    return returned.reshape(slots)[dest]


def solution(mesh):
    placed = (P(("grp", "mem"), None), P(("grp", "mem")), P(("grp", "mem")))
    return jax.shard_map(
        shards, mesh=mesh, in_specs=placed, out_specs=P(("grp", "mem")), check_vma=False
    )
```

profile of v0, /device:TPU:1, one launch (start us, length us, event | category | flops | bytes accessed | tf_op | source)
XLA Modules:
  0.0 162.1 jit_solution(17592987371388731186)
XLA Ops:
  6.5 0.0 all-gather.2.cloned.1.call-start
  6.5 1.4 fusion.1
  7.9 0.7 compare_select_fusion
  8.6 3.7 %scatter_custom_fusion.1 = bf16[1024,768]{1,0:T(8,128)(2,1)S(1)} fusion(s32[512]{0:T(512)S(1)} %get-tuple-element.5, bf16[512,768]{1,0:T(8,128)(2,1)} %param.3, f32[512]{0:T(512)S(1)} %add_rsqrt_fusion, bf16[]{:T(256)} %constant.2.clone.1), kind=kCustom, calls=%fused_computation.10 | custom fusion | flops 1179648 | bytes 2361346 | tf_op jit(solution)/shard_map/scatter | solution.py:32
  12.3 36.3 %all_to_all.21 = bf16[128,8,768]{2,1,0:T(8,128)(2,1)} all-to-all(bf16[128,8,768]{2,1,0:T(8,128)(2,1)S(1)} %bitcast.7), channel_id=1, replica_groups=mesh['grp'=16,'mem'=8] {'grp','mem'}, dimensions={0} | all-to-all | bytes 3145728 | tf_op jit(solution)/shard_map/all_to_all | solution.py:37
  48.6 0.0 all-gather.2.cloned.1.call-update
  48.6 3.8 %scatter_custom_fusion = bf16[1024]{0:T(1024)(128)(2,1)S(1)} fusion(s32[512]{0:T(512)S(1)} %get-tuple-element.5, bf16[512]{0:T(512)(128)(2,1)S(1)} %get-tuple-element.6, bf16[]{:T(256)} %constant.9.clone.1), kind=kCustom, calls=%fused_computation.19 | custom fusion | bytes 2050 | tf_op jit(solution)/shard_map/scatter | solution.py:33
  52.4 0.7 all_to_all.17
  53.2 4.3 %all-to-all-start = ((bf16[128,1,8]{2,1,0:T(2,128)(2,1)}), bf16[128,1,8]{2,1,0:T(2,128)(2,1)S(1)}, u32[]{:S(2)}, u32[]{:S(2)}) async-start(bf16[128,1,8]{2,1,0:T(2,128)(2,1)} %all_to_all.17), calls=%async_computation | async-start | bytes 131072 | tf_op jit(solution)/shard_map/all_to_all | solution.py:44
  57.4 9.9 %all-to-all-done = bf16[128,1,8]{2,1,0:T(2,128)(2,1)S(1)} async-done(((bf16[128,1,8]{2,1,0:T(2,128)(2,1)}), bf16[128,1,8]{2,1,0:T(2,128)(2,1)S(1)}, u32[]{:S(2)}, u32[]{:S(2)}) %all-to-all-start) | async-done | bytes 2080 | tf_op jit(solution)/shard_map/all_to_all | solution.py:44
  67.3 0.2 reduce
  67.5 0.1 eq.15
  67.6 12.1 %all_gather.6 = bf16[8192]{0:T(1024)(128)(2,1)S(1)} all-gather(bf16[1024]{0:T(1024)(128)(2,1)S(1)} %eq.15), channel_id=1, replica_groups=mesh['grp'=16,'mem'=8] {'mem'}, dimensions={0}, use_global_device_ids=true | all-gather | bytes 18432 | tf_op jit(solution)/shard_map/all_gather | solution.py:61
  79.7 33.6 %all-gather.2.cloned.1.call-done = bf16[8192,768]{1,0:T(8,128)(2,1)} async-done(((bf16[1024,768]{1,0:T(8,128)(2,1)}), bf16[8192,768]{1,0:T(8,128)(2,1)}) %all-gather.2.cloned.1.call-update) | async-done | bytes 12582928 | tf_op jit(solution)/shard_map/all_gather | solution.py:60
  113.3 18.7 %select_reduce_fusion = f32[1024]{0:T(1024)S(1)} fusion(bf16[8192,768]{1,0:T(8,128)(2,1)} %all-gather.2.cloned.1.call-done, s32[1024]{0:T(1024)S(1)} %iota_add_fusion, bf16[8192]{0:T(1024)(128)(2,1)S(1)} %all_gather.6, bf16[1024]{0:T(1024)(128)(2,1)S(1)} %eq.15, bf16[128,8,768]{2,1,0:T(8,128)(2,1)} %all_to_all.21), kind=kOutput, calls=%fused_computation.3 | convolution fusion | flops 12943621120 | bytes 14182400 | tf_op jit(solution)/shard_map/dot_general | solution.py:9
  132.1 0.7 max_broadcast_in_dim.15
  132.8 8.1 %all-to-all-start.2 = ((f32[128,1,8]{2,1,0:T(1,128)}), f32[128,1,8]{2,1,0:T(1,128)S(1)}, u32[]{:S(2)}, u32[]{:S(2)}) async-start(f32[128,1,8]{2,1,0:T(1,128)} %bitcast.2), calls=%async_computation.2 | async-start | bytes 131072 | tf_op jit(solution)/shard_map/all_to_all | solution.py:64
  140.9 9.5 %all-to-all-done.2 = f32[128,1,8]{2,1,0:T(1,128)S(1)} async-done(((f32[128,1,8]{2,1,0:T(1,128)}), f32[128,1,8]{2,1,0:T(1,128)S(1)}, u32[]{:S(2)}, u32[]{:S(2)}) %all-to-all-start.2) | async-done | bytes 4128 | tf_op jit(solution)/shard_map/all_to_all | solution.py:64
  150.4 0.5 broadcast.38
  150.9 0.8 reduce.4
  151.7 0.1 reshape.47
  151.8 3.4 %gather_fusion = f32[512]{0:T(512)} fusion(f32[1024]{0:T(1024)S(1)} %reshape.47, s32[1024]{0:T(1024)S(1)} %pad_clamp_fusion), kind=kCustom, calls=%fused_computation | custom fusion | bytes 6144 | tf_op jit(solution)/shard_map/gather | solution.py:67
  (4 shorter events, 0.0 us)
Async XLA Ops:
  6.5 106.8 %all-gather.2.cloned.1.call-start = ((), (), s32[]{:S(2)}) async-start(), calls=%async_computation.3 | async-start | bytes 14155776 | tf_op jit(solution)/shard_map/all_gather | solution.py:60
  53.2 14.2 %all-to-all-start = ((bf16[128,1,8]{2,1,0:T(2,128)(2,1)}), bf16[128,1,8]{2,1,0:T(2,128)(2,1)S(1)}, u32[]{:S(2)}, u32[]{:S(2)}) async-start(bf16[128,1,8]{2,1,0:T(2,128)(2,1)} %all_to_all.17), calls=%async_computation | async-start | bytes 131072 | tf_op jit(solution)/shard_map/all_to_all | solution.py:44
  132.8 17.6 %all-to-all-start.2 = ((f32[128,1,8]{2,1,0:T(1,128)}), f32[128,1,8]{2,1,0:T(1,128)S(1)}, u32[]{:S(2)}, u32[]{:S(2)}) async-start(f32[128,1,8]{2,1,0:T(1,128)} %bitcast.2), calls=%async_computation.2 | async-start | bytes 131072 | tf_op jit(solution)/shard_map/all_to_all | solution.py:64
Sparse Core Ops, SparseCore 0:
  48.8 64.4 all-gather.1
where the time goes:
time: 162 us
  waiting for transfers between devices  53 us (33%)
  blocking collectives  48.4 us (30%)
  matrix products  18.7 us (12%)
  between operations  13.5 us (8%)
  starting transfers between devices  12.4 us (8%)
  local copies, waits for them, and re-layouts  9.33 us (6%)
  other arithmetic  6.75 us (4%)
    all_to_all x1, blocking collectives, shards(): lax.all_to_all(outgoing.reshape(devices, capacity, width), ('grp', 'mem')...  36.3 us
    all_gather x1, waiting for transfers between devices, shards(): lax.all_gather(local, 'mem', axis=0, tiled=True)  33.6 us
    dot_general x1, matrix products, fold_with(): lax.dot_general(queries, columns, (((1,), (1,)), ((), ())), preferred_ele...  18.7 us
    all_gather x1, blocking collectives, shards(): lax.all_gather(local_labels, 'mem', axis=0, tiled=True)  12.1 us
    all_to_all x1, waiting for transfers between devices, shards(): lax.all_to_all(out_labels.reshape(devices, capacity), ('grp', 'mem'), spl...  9.87 us
    all_to_all x1, waiting for transfers between devices, shards(): lax.all_to_all(results.reshape(devices, capacity), ('grp', 'mem'), split_...  9.48 us
    all_to_all x1, starting transfers between devices, shards(): lax.all_to_all(results.reshape(devices, capacity), ('grp', 'mem'), split_...  8.13 us
    all_to_all x1, starting transfers between devices, shards(): lax.all_to_all(out_labels.reshape(devices, capacity), ('grp', 'mem'), spl...  4.26 us
  transfers between devices with their start and end apart: 3, of which 3 were waited for; matrix products, arithmetic and copies ran while one was open for 3% of the time, Pallas kernels for 0%

commit v1 on v0

v1 whole, which is shorter than its diff:
```python
import functools

import jax
import jax.numpy as jnp
from jax import lax
from jax.experimental import pallas as pl
from jax.experimental.pallas import tpu as pltpu
from jax.sharding import PartitionSpec as P

CAP = 8
SHARED = 2
LANES = 128
EMPTY = 2.0
VMEM_LIMIT = 48 * 1024 * 1024
HIGHEST = lax.Precision.HIGHEST


def params():
    return pltpu.CompilerParams(vmem_limit_bytes=VMEM_LIMIT)


def dot_t(a, b):
    return lax.dot_general(a, b, (((1,), (1,)), ((), ())), preferred_element_type=jnp.float32)


def pack_kernel(embeds_ref, cluster_ref, dest_ref, out_ref, unit_ref):
    rows, width = embeds_ref.shape
    block = out_ref.shape[0]

    @pl.when(pl.program_id(0) == 0)
    def _():
        values = embeds_ref[...].astype(jnp.float32)
        total = jnp.sum(values * values, axis=1, keepdims=True)
        unit_ref[...] = (values * lax.rsqrt(total + 1e-06)).astype(jnp.bfloat16)

    slot = pl.program_id(0) * block + lax.broadcasted_iota(jnp.int32, (block, rows), 0)
    here = slot == dest_ref[...]
    pick = jnp.where(here, 1.0, 0.0).astype(jnp.bfloat16)
    labels = (cluster_ref[...] + 1).astype(jnp.float32)
    marks = jnp.where(here, labels, 0.0).astype(jnp.bfloat16)
    out_ref[:, :width] = jnp.dot(
        pick, unit_ref[...], preferred_element_type=jnp.float32
    ).astype(jnp.bfloat16)
    out_ref[:, width:] = jnp.dot(
        marks, jnp.ones((rows, LANES), jnp.bfloat16), preferred_element_type=jnp.float32
    ).astype(jnp.bfloat16)


def pack(embeds, cluster, dest, slots):
    rows, width = embeds.shape
    block = 256
    whole = lambda i: (0, 0)
    return pl.pallas_call(
        pack_kernel,
        grid=(slots // block,),
        out_shape=jax.ShapeDtypeStruct((slots, width + LANES), jnp.bfloat16),
        in_specs=[
            pl.BlockSpec((rows, width), whole),
            pl.BlockSpec((1, rows), whole),
            pl.BlockSpec((1, rows), whole),
        ],
        out_specs=pl.BlockSpec((block, width + LANES), lambda i: (i, 0)),
        scratch_shapes=[pltpu.VMEM((rows, width), jnp.bfloat16)],
        compiler_params=params(),
    )(embeds, cluster.reshape(1, rows), dest.reshape(1, rows))


def extract_kernel(rows_ref, out_ref):
    slots, wide = rows_ref.shape
    width = wide - LANES
    chunk = out_ref.shape[0]
    sources = slots // CAP
    row = lax.broadcasted_iota(jnp.int32, (chunk, slots), 0)
    want = (row % sources) * CAP + row // sources
    pick = jnp.where(lax.broadcasted_iota(jnp.int32, (chunk, slots), 1) == want, 1.0, 0.0)
    pick = pick.astype(jnp.bfloat16)
    picked = jnp.dot(pick, rows_ref[...], preferred_element_type=jnp.float32)
    empty = (picked[:, width:] == 0.0) & (
        lax.broadcasted_iota(jnp.int32, (chunk, LANES), 1) == 0
    )
    out_ref[:, :LANES] = jnp.where(empty, EMPTY, picked[:, :LANES]).astype(jnp.bfloat16)
    out_ref[:, LANES:] = picked[:, LANES:width].astype(jnp.bfloat16)


def extract(arrived, chunk):
    slots, wide = arrived.shape
    return pl.pallas_call(
        extract_kernel,
        out_shape=jax.ShapeDtypeStruct((chunk, wide - LANES), jnp.bfloat16),
        compiler_params=params(),
    )(arrived)


def local_kernel(rows_ref, out_ref):
    slots, wide = rows_ref.shape
    width = wide - LANES
    block = 256
    column_labels = dot_t(jnp.ones((8, LANES), jnp.bfloat16), rows_ref[:, width:])[:1] * (
        1.0 / LANES
    )
    eye = lax.broadcasted_iota(jnp.int32, (block, block), 0) == lax.broadcasted_iota(
        jnp.int32, (block, block), 1
    )
    for q in range(slots // block):
        queries = rows_ref[q * block : (q + 1) * block, :width]
        labels = column_labels[:, q * block : (q + 1) * block]
        best = jnp.full((1, block), -1.0, jnp.float32)
        for k in range(slots // block):
            keys = rows_ref[k * block : (k + 1) * block, :]
            scores = dot_t(keys[:, :width], queries)
            key_labels = keys[:, width : width + 1].astype(jnp.float32)
            same = key_labels == labels
            if k == q:
                same = same & ~eye
            best = jnp.maximum(
                best, jnp.max(jnp.where(same, scores, -1.0), axis=0, keepdims=True)
            )
        out_ref[:, q * block : (q + 1) * block] = best


def local_best(arrived):
    slots, wide = arrived.shape
    return pl.pallas_call(
        local_kernel,
        out_shape=jax.ShapeDtypeStruct((1, slots), jnp.float32),
        compiler_params=params(),
    )(arrived)


def spread_kernel(members, place_ref, local_ref, own_ref, other_ref, after_ref, before_ref, out_ref):
    chunk = own_ref.shape[0]
    sources = chunk // SHARED

    def best(keys_ref, queries_ref):
        scores = dot_t(keys_ref[...], queries_ref[...])
        filled = keys_ref[:, :1].astype(jnp.float32) < (1.0 + EMPTY) / 2
        return jnp.max(jnp.where(filled, scores, -1.0), axis=0, keepdims=True)

    own = jnp.maximum(best(other_ref, own_ref), best(after_ref, own_ref))
    other = best(after_ref, other_ref)
    before = best(after_ref, before_ref)
    after = jnp.maximum(
        jnp.maximum(best(own_ref, after_ref), best(other_ref, after_ref)),
        best(before_ref, after_ref),
    )
    parts = []
    lanes = []
    for index, values in enumerate((own, other, after, before)):
        values = jnp.maximum(values, -1.0) + 1.0
        member = place_ref[index]
        for j in range(SHARED):
            parts.append(values[:, j * sources : (j + 1) * sources])
            lanes.append(CAP + SHARED * member + j)
    stacked = jnp.concatenate(parts, axis=0)
    row = lax.broadcasted_iota(jnp.int32, (len(parts), LANES), 0)
    lane = lax.broadcasted_iota(jnp.int32, (len(parts), LANES), 1)
    target = jnp.zeros((len(parts), LANES), jnp.int32)
    for index, value in enumerate(lanes):
        target = jnp.where(row == index, value, target)
    place = jnp.where(lane == target, 1.0, 0.0)
    table = lax.dot_general(
        stacked, place, (((0,), (0,)), ((), ())), precision=HIGHEST,
        preferred_element_type=jnp.float32,
    )

    per = LANES // CAP
    source = lax.broadcasted_iota(jnp.int32, (sources, LANES), 0)
    lane = lax.broadcasted_iota(jnp.int32, (sources, LANES), 1)
    spots = [
        jnp.broadcast_to(local_ref[:, t * LANES : (t + 1) * LANES], (per, LANES))
        for t in range(sources // per)
    ]
    mine = jnp.where(lane // CAP == source % per, jnp.concatenate(spots, axis=0) + 1.0, 0.0)
    fold = jnp.where(source % CAP == lane, 1.0, 0.0)
    table = table + jnp.dot(
        mine, fold, precision=HIGHEST, preferred_element_type=jnp.float32
    )
    out_ref[...] = table - 1.0


def spread_best(place, local, own, other, after, before, members):
    sources = own.shape[0] // SHARED
    vmem = pl.BlockSpec(memory_space=pltpu.VMEM)
    return pl.pallas_call(
        functools.partial(spread_kernel, members),
        out_shape=jax.ShapeDtypeStruct((sources, LANES), jnp.float32),
        in_specs=[pl.BlockSpec(memory_space=pltpu.SMEM)] + [vmem] * 5,
        compiler_params=params(),
    )(place, local, own, other, after, before)


def lookup_kernel(members, table_ref, dest_ref, out_ref):
    devices = table_ref.shape[0]
    rows = dest_ref.shape[1]
    table = table_ref[...]
    grouped = table.reshape(devices // members, members, LANES)
    most = jnp.broadcast_to(jnp.max(grouped, axis=1, keepdims=True), grouped.shape)
    lane = lax.broadcasted_iota(jnp.int32, (devices, LANES), 1)
    table = jnp.where(lane < CAP, table, most.reshape(devices, LANES))
    dest = dest_ref[...]
    owner = dest // CAP
    column = dest % CAP
    pick = jnp.where(
        lax.broadcasted_iota(jnp.int32, (devices, rows), 0) == owner, 1.0, 0.0
    )
    found = lax.dot_general(
        table, pick, (((0,), (0,)), ((), ())), precision=HIGHEST,
        preferred_element_type=jnp.float32,
    )
    lane = lax.broadcasted_iota(jnp.int32, (LANES, rows), 0)
    shared = jnp.where(column < SHARED, CAP + SHARED * (owner % members) + column, column)
    wanted = (lane == column) | (lane == shared)
    out_ref[...] = jnp.max(jnp.where(wanted, found, -1.0), axis=0, keepdims=True)


def lookup(table, dest, members):
    rows = dest.shape[0]
    return pl.pallas_call(
        functools.partial(lookup_kernel, members),
        out_shape=jax.ShapeDtypeStruct((1, rows), jnp.float32),
        compiler_params=params(),
    )(table, dest.reshape(1, rows)).reshape(rows)


def neighbours(members):
    chips = members // 2
    other, after, before = [], [], []
    for chip in range(chips):
        for core in range(2):
            other.append(2 * chip + 1 - core)
            after.append(2 * ((chip + 1) % chips) + core)
            crossed = core if chip < chips // 2 else 1 - core
            before.append(2 * ((chip - 1) % chips) + crossed)
    return other, after, before


def shards(embeds, cluster, dest):
    members = lax.axis_size("mem")
    devices = lax.axis_size("grp") * members
    width = embeds.shape[1]
    slots = devices * CAP
    outgoing = pack(embeds, cluster, dest, slots)
    arrived = lax.all_to_all(
        outgoing.reshape(devices, CAP, width + LANES),
        ("grp", "mem"),
        split_axis=0,
        concat_axis=0,
        tiled=True,
    ).reshape(slots, width + LANES)
    own = extract(arrived, devices * SHARED)
    sources = neighbours(members)
    received = [
        lax.ppermute(own, "mem", [(s, d) for d, s in enumerate(source)]) for source in sources
    ]
    local = local_best(arrived)
    me = lax.axis_index("mem")
    place = jnp.stack([me] + [jnp.asarray(s, jnp.int32)[me] for s in sources]).astype(jnp.int32)
    table = spread_best(place, local, own, *received, members)
    returned = lax.all_to_all(
        table.reshape(devices, 1, LANES),
        ("grp", "mem"),
        split_axis=0,
        concat_axis=0,
        tiled=True,
    ).reshape(devices, LANES)
    return lookup(returned, dest, members)


def solution(mesh):
    placed = (P(("grp", "mem"), None), P(("grp", "mem")), P(("grp", "mem")))
    return jax.shard_map(
        shards, mesh=mesh, in_specs=placed, out_specs=P(("grp", "mem")), check_vma=False
    )
```

time: 162 us -> 73.9 us (0.46)
  waiting for transfers between devices: 53 us -> 1.09 us
  matrix products: 18.7 us -> 0 us
  between operations: 13.5 us -> 0.05 us
  starting transfers between devices: 12.4 us -> 4.18 us
  Pallas kernels: 0 us -> 7.6 us
  blocking collectives: 48.4 us -> 54.4 us
  local copies, waits for them, and re-layouts: 9.33 us -> 4.4 us
  other arithmetic: 6.75 us -> 1.95 us
    all_gather x1 -> x0, waiting for transfers between devices: 33.6 us -> none  [shards(): lax.all_gather(local, 'mem', axis=0, tiled=True)]
    all_to_all x2 -> x0, waiting for transfers between devices: 19.4 us -> none  [the longest x1 9.87 us: shards(): lax.all_to_all(out_labels.reshape(devices, capacity), ('grp', 'mem'), spl...]
    dot_general x1 -> x0, matrix products: 18.7 us -> none  [fold_with(): lax.dot_general(queries, columns, (((1,), (1,)), ((), ())), preferred_ele...]
    all_to_all x1 -> x2, blocking collectives: 36.3 us -> 54.4 us  [the longest x1 39.1 us: shards(): lax.all_to_all(outgoing.reshape(devices, CAP, width + LANES), ('grp', 'me...]
    all_to_all x2 -> x0, starting transfers between devices: 12.4 us -> none  [the longest x1 8.13 us: shards(): lax.all_to_all(results.reshape(devices, capacity), ('grp', 'mem'), split_...]
    all_gather x1 -> x0, blocking collectives: 12.1 us -> none  [shards(): lax.all_gather(local_labels, 'mem', axis=0, tiled=True)]
    pallas_call x0 -> x5, Pallas kernels: none -> 7.6 us  [the longest x1 2.05 us: pack(): pl.pallas_call(pack_kernel, grid=(slots // block,), out_shape=jax.ShapeDt...]
    ppermute x0 -> x3, starting transfers between devices: none -> 4.18 us  [shards(): lax.ppermute(own, 'mem', [(s, d) for d, s in enumerate(source)])]
  transfers between devices with their start and end apart: 3 -> 3, of which waited for: 3 -> 1; matrix products, arithmetic and copies ran while one was open for 3% -> 5% of each run, Pallas kernels for 0% -> 3%
where the time goes in v1:
time: 73.9 us; the launch traced here: 73.6 us
  blocking collectives  54.4 us (74%)
  Pallas kernels  7.6 us (10%)
  local copies, waits for them, and re-layouts  4.4 us (6%)
  starting transfers between devices  4.18 us (6%)
  other arithmetic  1.95 us (3%)
  waiting for transfers between devices  1.09 us (1%)
    all_to_all x1, blocking collectives, shards(): lax.all_to_all(outgoing.reshape(devices, CAP, width + LANES), ('grp', 'me...  39.1 us
    all_to_all x1, blocking collectives, shards(): lax.all_to_all(table.reshape(devices, 1, LANES), ('grp', 'mem'), split_ax...  15.3 us
    ppermute x3, starting transfers between devices, shards(): lax.ppermute(own, 'mem', [(s, d) for d, s in enumerate(source)])  4.18 us
    unnamed x14, local copies, waits for them, and re-layouts  2.51 us
    pallas_call x1, Pallas kernels, pack(): pl.pallas_call(pack_kernel, grid=(slots // block,), out_shape=jax.ShapeDt...  2.05 us
    another operation x1, other arithmetic, shards(): jnp.stack([me] + [jnp.asarray(s, jnp.int32)[me] for s in sources])  1.95 us
    pallas_call x1, Pallas kernels, local_best(): pl.pallas_call(local_kernel, out_shape=jax.ShapeDtypeStruct((1, slots), j...  1.92 us
    dynamic_slice x3, local copies, waits for them, and re-layouts, shards(): jnp.asarray(s, jnp.int32)[me]  1.89 us
  transfers between devices with their start and end apart: 3, of which 1 were waited for; matrix products, arithmetic and copies ran while one was open for 5% of the time, Pallas kernels for 3%

profile of v1, /device:TPU:1, one launch (start us, length us, event | category | flops | bytes accessed | tf_op | source)
XLA Modules:
  0.0 73.6 jit_solution(5730404542810190877)
XLA Ops:
  0.0 0.0 copy-start
  0.0 1.1 %copy-done = bf16[512,768]{1,0:T(8,128)(2,1)S(1)} copy-done((bf16[512,768]{1,0:T(8,128)(2,1)S(1)}, bf16[512,768]{1,0:T(8,128)(2,1)}, u32[]{:S(2)}) %copy-start) | copy-done | bytes 786456
  1.1 0.0 copy-start.1
  1.1 0.7 copy-done.1
  1.8 0.0 copy-start.3
  1.8 0.7 copy-done.3
  2.5 2.0 %shard_map.64 = bf16[1024,896]{1,0:T(8,128)(2,1)S(1)} custom-call(bf16[512,768]{1,0:T(8,128)(2,1)S(1)} %copy-done, s32[1,512]{1,0:T(1,128)S(1)} %bitcast.17, s32[1,512]{1,0:T(1,128)S(1)} %bitcast.15), custom_call_target="tpu_custom_call" | custom-call | tf_op jit(solution)/shard_map/pallas_call | solution.py:53
  4.6 39.1 %all_to_all.10 = bf16[128,8,896]{2,1,0:T(8,128)(2,1)S(1)} all-to-all(bf16[128,8,896]{2,1,0:T(8,128)(2,1)S(1)} %bitcast.12), channel_id=1, replica_groups=mesh['grp'=16,'mem'=8] {'grp','mem'}, dimensions={0} | all-to-all | bytes 3670016 | tf_op jit(solution)/shard_map/all_to_all | solution.py:243
  43.6 0.0 copy-start.6
  43.6 0.0 copy-start.5
  43.6 0.0 copy-start.4
  43.6 0.7 shard_map.66.own_ref
  44.4 0.0 copy-start.2
  44.4 0.1 collective-permute-start.2
  44.5 2.7 %collective-permute-start.1 = (bf16[256,768]{1,0:T(8,128)(2,1)S(1)}, bf16[256,768]{1,0:T(8,128)(2,1)S(1)}, u32[]{:S(2)}, u32[]{:S(2)}) collective-permute-start(bf16[256,768]{1,0:T(8,128)(2,1)S(1)} %shard_map.66.own_ref), channel_id=1, source_target_pairs={{2,0},{3,1},{4,2},{5,3},{6,4},{7,5},{0,6},{1,7},{10,8},{11,9},{12,... | collective-permute-start | bytes 1179656 | tf_op jit(solution)/shard_map/ppermute | solution.py:253
  47.1 1.4 %collective-permute-start = (bf16[256,768]{1,0:T(8,128)(2,1)S(1)}, bf16[256,768]{1,0:T(8,128)(2,1)S(1)}, u32[]{:S(2)}, u32[]{:S(2)}) collective-permute-start(bf16[256,768]{1,0:T(8,128)(2,1)S(1)} %shard_map.66.own_ref), channel_id=1, source_target_pairs={{1,0},{0,1},{3,2},{2,3},{5,4},{4,5},{7,6},{6,7},{9,8},{8,9},{11,10... | collective-permute-start | bytes 1179656 | tf_op jit(solution)/shard_map/ppermute | solution.py:253
  48.6 0.0 copy-done.6
  48.6 0.6 dynamic_slice.11
  49.2 0.0 copy-done.5
  49.2 0.6 dynamic_slice.10
  49.8 0.0 copy-done.4
  49.8 0.6 dynamic_slice.9
  50.5 2.0 %pad_add_fusion.place_ref = s32[4]{0:T(128)S(1)} fusion(s32[1]{0:T(128)} %dynamic_slice.11, s32[1]{0:T(128)} %dynamic_slice.10, s32[1]{0:T(128)} %dynamic_slice.9, s32[1]{0:T(128)} %bitcast), kind=kLoop, calls=%fused_computation | loop fusion | flops 12 | bytes 32 | tf_op jit(solution)/shard_map/stack | solution.py:257
  52.4 1.9 %shard_map.65.local_ref = f32[1,1024]{1,0:T(1,128)S(1)} custom-call(bf16[1024,896]{1,0:T(8,128)(2,1)S(1)} %bitcast.11), custom_call_target="tpu_custom_call" | custom-call | tf_op jit(solution)/shard_map/pallas_call | solution.py:123
  54.3 1.1 %collective-permute-done.2.before_ref = bf16[256,768]{1,0:T(8,128)(2,1)S(1)} collective-permute-done((bf16[256,768]{1,0:T(8,128)(2,1)S(1)}, bf16[256,768]{1,0:T(8,128)(2,1)S(1)}, u32[]{:S(2)}, u32[]{:S(2)}) %collective-permute-start.2) | collective-permute-done | bytes 393248 | tf_op jit(solution)/shard_map/ppermute | solution.py:253
  55.4 0.0 collective-permute-done.1.after_ref
  55.4 0.0 collective-permute-done.other_ref
  55.4 1.9 %shard_map.67 = f32[128,128]{1,0:T(8,128)S(1)} custom-call(s32[4]{0:T(128)S(1)} %pad_add_fusion.place_ref, f32[1,1024]{1,0:T(1,128)S(1)} %shard_map.65.local_ref, bf16[256,768]{1,0:T(8,128)(2,1)S(1)} %shard_map.66.own_ref, bf16[256,768]{1,0:T(8,128)(2,1)S(1)} %collective-permute-done.other_ref, bf16[256,768]{1,0:T(8,128)(2,1)S(1)} %collective-permute-done.1.after_ref, ...), custom_call_target="tpu_custom_call" | custom-call | tf_op jit(solution)/shard_map/pallas_call | solution.py:184
  57.3 15.3 %all_to_all.11 = f32[128,1,128]{2,1,0:T(1,128)S(1)} all-to-all(f32[128,1,128]{2,1,0:T(1,128)S(1)} %bitcast.13), channel_id=1, replica_groups=mesh['grp'=16,'mem'=8] {'grp','mem'}, dimensions={0} | all-to-all | bytes 131072 | tf_op jit(solution)/shard_map/all_to_all | solution.py:259
  72.6 0.0 copy-done.2
  72.6 1.1 %shard_map.68 = f32[1,512]{1,0:T(1,128)} custom-call(f32[128,128]{1,0:T(8,128)S(1)} %bitcast.14, s32[1,512]{1,0:T(1,128)S(1)} %bitcast.16), custom_call_target="tpu_custom_call" | custom-call | tf_op jit(solution)/shard_map/pallas_call | solution.py:218
Async XLA Ops:
  0.0 1.1 %copy-start = (bf16[512,768]{1,0:T(8,128)(2,1)S(1)}, bf16[512,768]{1,0:T(8,128)(2,1)}, u32[]{:S(2)}) copy-start(bf16[512,768]{1,0:T(8,128)(2,1)} %embeds_ref.1) | copy-start | bytes 2359300
  1.1 0.7 copy-start.1
  1.8 0.7 copy-start.3
  43.6 4.9 %copy-start.6 = (s32[8]{0:T(128)S(1)}, s32[8]{0:T(128)}, u32[]{:S(2)}) copy-start(s32[8]{0:T(128)} %constant.16.clone) | copy-start | bytes 100
  43.6 5.6 %copy-start.5 = (s32[8]{0:T(128)S(1)}, s32[8]{0:T(128)}, u32[]{:S(2)}) copy-start(s32[8]{0:T(128)} %constant.15.clone) | copy-start | bytes 100
  43.6 6.2 %copy-start.4 = (s32[8]{0:T(128)S(1)}, s32[8]{0:T(128)}, u32[]{:S(2)}) copy-start(s32[8]{0:T(128)} %constant.14.clone) | copy-start | bytes 100
  44.4 28.2 %copy-start.2 = (s32[512]{0:T(512)S(1)}, s32[512]{0:T(512)}, u32[]{:S(2)}) copy-start(s32[512]{0:T(512)} %param.8) | copy-start | bytes 6148
  44.4 11.0 %collective-permute-start.2 = (bf16[256,768]{1,0:T(8,128)(2,1)S(1)}, bf16[256,768]{1,0:T(8,128)(2,1)S(1)}, u32[]{:S(2)}, u32[]{:S(2)}) collective-permute-start(bf16[256,768]{1,0:T(8,128)(2,1)S(1)} %shard_map.66.own_ref), channel_id=1, source_target_pairs={{6,0},{7,1},{0,2},{1,3},{3,4},{2,5},{5,6},{4,7},{14,8},{15,9},{8,1... | collective-permute-start | bytes 1179656 | tf_op jit(solution)/shard_map/ppermute | solution.py:253
  44.5 11.0 %collective-permute-start.1 = (bf16[256,768]{1,0:T(8,128)(2,1)S(1)}, bf16[256,768]{1,0:T(8,128)(2,1)S(1)}, u32[]{:S(2)}, u32[]{:S(2)}) collective-permute-start(bf16[256,768]{1,0:T(8,128)(2,1)S(1)} %shard_map.66.own_ref), channel_id=1, source_target_pairs={{2,0},{3,1},{4,2},{5,3},{6,4},{7,5},{0,6},{1,7},{10,8},{11,9},{12,... | collective-permute-start | bytes 1179656 | tf_op jit(solution)/shard_map/ppermute | solution.py:253
  47.1 8.3 %collective-permute-start = (bf16[256,768]{1,0:T(8,128)(2,1)S(1)}, bf16[256,768]{1,0:T(8,128)(2,1)S(1)}, u32[]{:S(2)}, u32[]{:S(2)}) collective-permute-start(bf16[256,768]{1,0:T(8,128)(2,1)S(1)} %shard_map.66.own_ref), channel_id=1, source_target_pairs={{1,0},{0,1},{3,2},{2,3},{5,4},{4,5},{7,6},{6,7},{9,8},{8,9},{11,10... | collective-permute-start | bytes 1179656 | tf_op jit(solution)/shard_map/ppermute | solution.py:253

commit v2 on v1

--- a/solution.py
+++ b/solution.py
@@ -10,6 +10,7 @@
 CAP = 8
 SHARED = 2
 LANES = 128
+PARTS = 4
 EMPTY = 2.0
 VMEM_LIMIT = 48 * 1024 * 1024
 HIGHEST = lax.Precision.HIGHEST
@@ -23,44 +24,64 @@
     return lax.dot_general(a, b, (((1,), (1,)), ((), ())), preferred_element_type=jnp.float32)
 
 
-def pack_kernel(embeds_ref, cluster_ref, dest_ref, out_ref, unit_ref):
+def pack_kernel(embeds_hbm, cluster_hbm, dest_hbm, out_ref, embeds_ref, cluster_ref, dest_ref, unit_ref, sems):
     rows, width = embeds_ref.shape
-    block = out_ref.shape[0]
-
-    @pl.when(pl.program_id(0) == 0)
-    def _():
-        values = embeds_ref[...].astype(jnp.float32)
+    slots = out_ref.shape[0]
+    part = rows // PARTS
+    small = [
+        pltpu.make_async_copy(dest_hbm, dest_ref, sems.at[0]),
+        pltpu.make_async_copy(cluster_hbm, cluster_ref, sems.at[1]),
+    ]
+    large = [
+        pltpu.make_async_copy(
+            embeds_hbm.at[pl.ds(p * part, part)],
+            embeds_ref.at[pl.ds(p * part, part)],
+            sems.at[2 + p],
+        )
+        for p in range(PARTS)
+    ]
+    for copy in small + large:
+        copy.start()
+    for copy in small:
+        copy.wait()
+    labels = jnp.broadcast_to((cluster_ref[...] + 1).astype(jnp.float32), (8, rows))
+    first = lax.broadcasted_iota(jnp.int32, (8, rows), 0) == 0
+    labels = jnp.where(first, labels, 0.0).astype(jnp.bfloat16)
+    unit_ref[:, width:] = lax.dot_general(
+        labels, jnp.ones((8, LANES), jnp.bfloat16), (((0,), (0,)), ((), ())),
+        preferred_element_type=jnp.float32,
+    ).astype(jnp.bfloat16)
+    block = 256
+    picks = []
+    for b in range(slots // block):
+        slot = b * block + lax.broadcasted_iota(jnp.int32, (block, rows), 0)
+        picks.append(jnp.where(slot == dest_ref[...], 1.0, 0.0).astype(jnp.bfloat16))
+    for p in range(PARTS):
+        large[p].wait()
+        values = embeds_ref[p * part : (p + 1) * part, :].astype(jnp.float32)
         total = jnp.sum(values * values, axis=1, keepdims=True)
-        unit_ref[...] = (values * lax.rsqrt(total + 1e-06)).astype(jnp.bfloat16)
-
-    slot = pl.program_id(0) * block + lax.broadcasted_iota(jnp.int32, (block, rows), 0)
-    here = slot == dest_ref[...]
-    pick = jnp.where(here, 1.0, 0.0).astype(jnp.bfloat16)
-    labels = (cluster_ref[...] + 1).astype(jnp.float32)
-    marks = jnp.where(here, labels, 0.0).astype(jnp.bfloat16)
-    out_ref[:, :width] = jnp.dot(
-        pick, unit_ref[...], preferred_element_type=jnp.float32
-    ).astype(jnp.bfloat16)
-    out_ref[:, width:] = jnp.dot(
-        marks, jnp.ones((rows, LANES), jnp.bfloat16), preferred_element_type=jnp.float32
-    ).astype(jnp.bfloat16)
+        unit_ref[p * part : (p + 1) * part, :width] = (
+            values * lax.rsqrt(total + 1e-06)
+        ).astype(jnp.bfloat16)
+    for b in range(slots // block):
+        out_ref[b * block : (b + 1) * block, :] = jnp.dot(
+            picks[b], unit_ref[...], preferred_element_type=jnp.float32
+        ).astype(jnp.bfloat16)
 
 
 def pack(embeds, cluster, dest, slots):
     rows, width = embeds.shape
-    block = 256
-    whole = lambda i: (0, 0)
     return pl.pallas_call(
         pack_kernel,
-        grid=(slots // block,),
         out_shape=jax.ShapeDtypeStruct((slots, width + LANES), jnp.bfloat16),
-        in_specs=[
-            pl.BlockSpec((rows, width), whole),
-            pl.BlockSpec((1, rows), whole),
-            pl.BlockSpec((1, rows), whole),
+        in_specs=[pl.BlockSpec(memory_space=pltpu.HBM)] * 3,
+        scratch_shapes=[
+            pltpu.VMEM((rows, width), jnp.bfloat16),
+            pltpu.VMEM((1, rows), jnp.int32),
+            pltpu.VMEM((1, rows), jnp.int32),
+            pltpu.VMEM((rows, width + LANES), jnp.bfloat16),
+            pltpu.SemaphoreType.DMA((2 + PARTS,)),
         ],
-        out_specs=pl.BlockSpec((block, width + LANES), lambda i: (i, 0)),
-        scratch_shapes=[pltpu.VMEM((rows, width), jnp.bfloat16)],
         compiler_params=params(),
     )(embeds, cluster.reshape(1, rows), dest.reshape(1, rows))
 
@@ -101,6 +122,7 @@
     eye = lax.broadcasted_iota(jnp.int32, (block, block), 0) == lax.broadcasted_iota(
         jnp.int32, (block, block), 1
     )
+    results = []
     for q in range(slots // block):
         queries = rows_ref[q * block : (q + 1) * block, :width]
         labels = column_labels[:, q * block : (q + 1) * block]
@@ -115,19 +137,33 @@
             best = jnp.maximum(
                 best, jnp.max(jnp.where(same, scores, -1.0), axis=0, keepdims=True)
             )
-        out_ref[:, q * block : (q + 1) * block] = best
+        results.append(best)
+    local = jnp.concatenate(results, axis=1)
+    sources = slots // CAP
+    per = LANES // CAP
+    source = lax.broadcasted_iota(jnp.int32, (sources, LANES), 0)
+    lane = lax.broadcasted_iota(jnp.int32, (sources, LANES), 1)
+    spots = [
+        jnp.broadcast_to(local[:, t * LANES : (t + 1) * LANES], (per, LANES))
+        for t in range(sources // per)
+    ]
+    mine = jnp.where(lane // CAP == source % per, jnp.concatenate(spots, axis=0) + 1.0, 0.0)
+    fold = jnp.where(source % CAP == lane, 1.0, 0.0)
+    out_ref[...] = jnp.dot(
+        mine, fold, precision=HIGHEST, preferred_element_type=jnp.float32
+    ) - 1.0
 
 
 def local_best(arrived):
     slots, wide = arrived.shape
     return pl.pallas_call(
         local_kernel,
-        out_shape=jax.ShapeDtypeStruct((1, slots), jnp.float32),
+        out_shape=jax.ShapeDtypeStruct((slots // CAP, LANES), jnp.float32),
         compiler_params=params(),
     )(arrived)
 
 
-def spread_kernel(members, place_ref, local_ref, own_ref, other_ref, after_ref, before_ref, out_ref):
+def spread_kernel(members, local_ref, own_ref, other_ref, after_ref, before_ref, out_ref):
     chunk = own_ref.shape[0]
     sources = chunk // SHARED
 
@@ -143,11 +179,12 @@
         jnp.maximum(best(own_ref, after_ref), best(other_ref, after_ref)),
         best(before_ref, after_ref),
     )
+    places = held(lax.axis_index("mem"), members)
     parts = []
     lanes = []
     for index, values in enumerate((own, other, after, before)):
         values = jnp.maximum(values, -1.0) + 1.0
-        member = place_ref[index]
+        member = places[index]
         for j in range(SHARED):
             parts.append(values[:, j * sources : (j + 1) * sources])
             lanes.append(CAP + SHARED * member + j)
@@ -163,30 +200,18 @@
         preferred_element_type=jnp.float32,
     )
 
-    per = LANES // CAP
-    source = lax.broadcasted_iota(jnp.int32, (sources, LANES), 0)
-    lane = lax.broadcasted_iota(jnp.int32, (sources, LANES), 1)
-    spots = [
-        jnp.broadcast_to(local_ref[:, t * LANES : (t + 1) * LANES], (per, LANES))
-        for t in range(sources // per)
-    ]
-    mine = jnp.where(lane // CAP == source % per, jnp.concatenate(spots, axis=0) + 1.0, 0.0)
-    fold = jnp.where(source % CAP == lane, 1.0, 0.0)
-    table = table + jnp.dot(
-        mine, fold, precision=HIGHEST, preferred_element_type=jnp.float32
-    )
-    out_ref[...] = table - 1.0
-
-
-def spread_best(place, local, own, other, after, before, members):
+    out_ref[...] = table + local_ref[...]
+
+
+def spread_best(local, own, other, after, before, members):
     sources = own.shape[0] // SHARED
     vmem = pl.BlockSpec(memory_space=pltpu.VMEM)
     return pl.pallas_call(
         functools.partial(spread_kernel, members),
         out_shape=jax.ShapeDtypeStruct((sources, LANES), jnp.float32),
-        in_specs=[pl.BlockSpec(memory_space=pltpu.SMEM)] + [vmem] * 5,
-        compiler_params=params(),
-    )(place, local, own, other, after, before)
+        in_specs=[vmem] * 5,
+        compiler_params=params(),
+    )(local, own, other, after, before)
 
 
 def lookup_kernel(members, table_ref, dest_ref, out_ref):
@@ -222,16 +247,16 @@
     )(table, dest.reshape(1, rows)).reshape(rows)
 
 
-def neighbours(members):
+def held(me, members):
     chips = members // 2
-    other, after, before = [], [], []
-    for chip in range(chips):
-        for core in range(2):
-            other.append(2 * chip + 1 - core)
-            after.append(2 * ((chip + 1) % chips) + core)
-            crossed = core if chip < chips // 2 else 1 - core
-            before.append(2 * ((chip - 1) % chips) + crossed)
-    return other, after, before
+    chip, core = me // 2, me % 2
+    crossed = (chip // (chips // 2) + core) % 2
+    return (
+        me,
+        2 * chip + 1 - core,
+        2 * ((chip + 1) % chips) + core,
+        2 * ((chip + chips - 1) % chips) + crossed,
+    )
 
 
 def shards(embeds, cluster, dest):
@@ -248,14 +273,12 @@
         tiled=True,
     ).reshape(slots, width + LANES)
     own = extract(arrived, devices * SHARED)
-    sources = neighbours(members)
     received = [
-        lax.ppermute(own, "mem", [(s, d) for d, s in enumerate(source)]) for source in sources
+        lax.ppermute(own, "mem", [(held(m, members)[i], m) for m in range(members)])
+        for i in (1, 2, 3)
     ]
     local = local_best(arrived)
-    me = lax.axis_index("mem")
-    place = jnp.stack([me] + [jnp.asarray(s, jnp.int32)[me] for s in sources]).astype(jnp.int32)
-    table = spread_best(place, local, own, *received, members)
+    table = spread_best(local, own, *received, members)
     returned = lax.all_to_all(
         table.reshape(devices, 1, LANES),
         ("grp", "mem"),

time: 73.9 us -> 74.4 us (level)
  waiting for transfers between devices: 1.09 us -> 4.74 us
  other arithmetic: 1.95 us -> 0 us
  local copies, waits for them, and re-layouts: 4.4 us -> 2.49 us
  Pallas kernels: 7.6 us -> 8.38 us
    ppermute x3, waiting for transfers between devices: 1.09 us -> 4.74 us  [shards(): lax.ppermute(own, 'mem', [(held(m, members)[i], m) for m in range(members)])]
    another operation x1 -> x0, other arithmetic: 1.95 us -> none  [shards(): jnp.stack([me] + [jnp.asarray(s, jnp.int32)[me] for s in sources])]
    dynamic_slice x3 -> x0, local copies, waits for them, and re-layouts: 1.89 us -> none  [shards(): jnp.asarray(s, jnp.int32)[me]]
    pallas_call x2, Pallas kernels: 3.97 us -> 5.34 us  [the longest x1 3.21 us: pack(): pl.pallas_call(pack_kernel, out_shape=jax.ShapeDtypeStruct((slots, width...]
    unnamed x14 -> x6, local copies, waits for them, and re-layouts: 2.51 us -> 2.49 us
  transfers between devices with their start and end apart: 3 -> 3, of which waited for: 1 -> 1; matrix products, arithmetic and copies ran while one was open for 5% -> 0% of each run, Pallas kernels for 3% -> 3%
where the time goes in v2:
time: 74.4 us; the launch traced here: 74.2 us
  blocking collectives  54.4 us (73%)
  Pallas kernels  8.38 us (11%)
  waiting for transfers between devices  4.74 us (6%)
  starting transfers between devices  4.17 us (6%)
  local copies, waits for them, and re-layouts  2.49 us (3%)
    all_to_all x1, blocking collectives, shards(): lax.all_to_all(outgoing.reshape(devices, CAP, width + LANES), ('grp', 'me...  39.1 us
    all_to_all x1, blocking collectives, shards(): lax.all_to_all(table.reshape(devices, 1, LANES), ('grp', 'mem'), split_ax...  15.3 us
    ppermute x3, waiting for transfers between devices, shards(): lax.ppermute(own, 'mem', [(held(m, members)[i], m) for m in range(members)])  4.74 us
    ppermute x3, starting transfers between devices, shards(): lax.ppermute(own, 'mem', [(held(m, members)[i], m) for m in range(members)])  4.17 us
    pallas_call x1, Pallas kernels, pack(): pl.pallas_call(pack_kernel, out_shape=jax.ShapeDtypeStruct((slots, width...  3.21 us
    unnamed x6, local copies, waits for them, and re-layouts  2.49 us
    pallas_call x1, Pallas kernels, local_best(): pl.pallas_call(local_kernel, out_shape=jax.ShapeDtypeStruct((slots // CAP...  2.13 us
  transfers between devices with their start and end apart: 3, of which 1 were waited for; matrix products, arithmetic and copies ran while one was open for 0% of the time, Pallas kernels for 3%

profile of v2, /device:TPU:1, one launch (start us, length us, event | category | flops | bytes accessed | tf_op | source)
XLA Modules:
  0.0 74.2 jit_solution(7597201086115759918)
XLA Ops:
  0.0 0.0 copy-start
  0.0 1.1 %copy-done = bf16[512,768]{1,0:T(8,128)(2,1)S(1)} copy-done((bf16[512,768]{1,0:T(8,128)(2,1)S(1)}, bf16[512,768]{1,0:T(8,128)(2,1)}, u32[]{:S(2)}) %copy-start) | copy-done | bytes 786456
  1.1 0.0 copy-start.1
  1.1 0.7 copy-done.1
  1.8 0.0 copy-start.2
  1.8 0.7 copy-done.2
  2.5 3.2 %shard_map.37 = bf16[1024,896]{1,0:T(8,128)(2,1)S(1)} custom-call(bf16[512,768]{1,0:T(8,128)(2,1)S(1)} %copy-done, s32[1,512]{1,0:T(1,128)S(1)} %bitcast.16, s32[1,512]{1,0:T(1,128)S(1)} %bitcast.14), custom_call_target="tpu_custom_call" | custom-call | tf_op jit(solution)/shard_map/pallas_call | solution.py:74
  5.7 39.1 %all_to_all.10 = bf16[128,8,896]{2,1,0:T(8,128)(2,1)S(1)} all-to-all(bf16[128,8,896]{2,1,0:T(8,128)(2,1)S(1)} %bitcast.11), channel_id=1, replica_groups=mesh['grp'=16,'mem'=8] {'grp','mem'}, dimensions={0} | all-to-all | bytes 3670016 | tf_op jit(solution)/shard_map/all_to_all | solution.py:268
  44.8 0.7 shard_map.39.own_ref
  45.5 0.1 collective-permute-start.2
  45.6 2.7 %collective-permute-start.1 = (bf16[256,768]{1,0:T(8,128)(2,1)S(1)}, bf16[256,768]{1,0:T(8,128)(2,1)S(1)}, u32[]{:S(2)}, u32[]{:S(2)}) collective-permute-start(bf16[256,768]{1,0:T(8,128)(2,1)S(1)} %shard_map.39.own_ref), channel_id=1, source_target_pairs={{2,0},{3,1},{4,2},{5,3},{6,4},{7,5},{0,6},{1,7},{10,8},{11,9},{12,... | collective-permute-start | bytes 1179656 | tf_op jit(solution)/shard_map/ppermute | solution.py:277
  48.3 1.4 %collective-permute-start = (bf16[256,768]{1,0:T(8,128)(2,1)S(1)}, bf16[256,768]{1,0:T(8,128)(2,1)S(1)}, u32[]{:S(2)}, u32[]{:S(2)}) collective-permute-start(bf16[256,768]{1,0:T(8,128)(2,1)S(1)} %shard_map.39.own_ref), channel_id=1, source_target_pairs={{1,0},{0,1},{3,2},{2,3},{5,4},{4,5},{7,6},{6,7},{9,8},{8,9},{11,10... | collective-permute-start | bytes 1179656 | tf_op jit(solution)/shard_map/ppermute | solution.py:277
  49.7 2.1 %shard_map.38.local_ref = f32[128,128]{1,0:T(8,128)S(1)} custom-call(bf16[1024,896]{1,0:T(8,128)(2,1)S(1)} %bitcast.10), custom_call_target="tpu_custom_call" | custom-call | tf_op jit(solution)/shard_map/pallas_call | solution.py:159
  51.8 4.7 %collective-permute-done.2.before_ref = bf16[256,768]{1,0:T(8,128)(2,1)S(1)} collective-permute-done((bf16[256,768]{1,0:T(8,128)(2,1)S(1)}, bf16[256,768]{1,0:T(8,128)(2,1)S(1)}, u32[]{:S(2)}, u32[]{:S(2)}) %collective-permute-start.2) | collective-permute-done | bytes 393248 | tf_op jit(solution)/shard_map/ppermute | solution.py:277
  56.6 0.0 collective-permute-done.1.after_ref
  56.6 0.0 collective-permute-done.other_ref
  56.6 1.3 %shard_map.40 = f32[128,128]{1,0:T(8,128)S(1)} custom-call(f32[128,128]{1,0:T(8,128)S(1)} %shard_map.38.local_ref, bf16[256,768]{1,0:T(8,128)(2,1)S(1)} %shard_map.39.own_ref, bf16[256,768]{1,0:T(8,128)(2,1)S(1)} %collective-permute-done.other_ref, bf16[256,768]{1,0:T(8,128)(2,1)S(1)} %collective-permute-done.1.after_ref, ...), custom_call_target="tpu_custom_call" | custom-call | tf_op jit(solution)/shard_map/pallas_call | solution.py:209
  57.9 15.3 %all_to_all.11 = f32[128,1,128]{2,1,0:T(1,128)S(1)} all-to-all(f32[128,1,128]{2,1,0:T(1,128)S(1)} %bitcast.13), channel_id=1, replica_groups=mesh['grp'=16,'mem'=8] {'grp','mem'}, dimensions={0} | all-to-all | bytes 131072 | tf_op jit(solution)/shard_map/all_to_all | solution.py:282
  73.1 1.1 %shard_map.41 = f32[1,512]{1,0:T(1,128)} custom-call(f32[128,128]{1,0:T(8,128)S(1)} %bitcast.12, s32[1,512]{1,0:T(1,128)S(1)} %bitcast.15), custom_call_target="tpu_custom_call" | custom-call | tf_op jit(solution)/shard_map/pallas_call | solution.py:243
Async XLA Ops:
  0.0 1.1 %copy-start = (bf16[512,768]{1,0:T(8,128)(2,1)S(1)}, bf16[512,768]{1,0:T(8,128)(2,1)}, u32[]{:S(2)}) copy-start(bf16[512,768]{1,0:T(8,128)(2,1)} %embeds_hbm.1) | copy-start | bytes 2359300
  1.1 0.7 copy-start.1
  1.8 0.7 copy-start.2
  45.5 11.0 %collective-permute-start.2 = (bf16[256,768]{1,0:T(8,128)(2,1)S(1)}, bf16[256,768]{1,0:T(8,128)(2,1)S(1)}, u32[]{:S(2)}, u32[]{:S(2)}) collective-permute-start(bf16[256,768]{1,0:T(8,128)(2,1)S(1)} %shard_map.39.own_ref), channel_id=1, source_target_pairs={{6,0},{7,1},{0,2},{1,3},{3,4},{2,5},{5,6},{4,7},{14,8},{15,9},{8,1... | collective-permute-start | bytes 1179656 | tf_op jit(solution)/shard_map/ppermute | solution.py:277
  45.6 11.0 %collective-permute-start.1 = (bf16[256,768]{1,0:T(8,128)(2,1)S(1)}, bf16[256,768]{1,0:T(8,128)(2,1)S(1)}, u32[]{:S(2)}, u32[]{:S(2)}) collective-permute-start(bf16[256,768]{1,0:T(8,128)(2,1)S(1)} %shard_map.39.own_ref), channel_id=1, source_target_pairs={{2,0},{3,1},{4,2},{5,3},{6,4},{7,5},{0,6},{1,7},{10,8},{11,9},{12,... | collective-permute-start | bytes 1179656 | tf_op jit(solution)/shard_map/ppermute | solution.py:277
  48.3 8.3 %collective-permute-start = (bf16[256,768]{1,0:T(8,128)(2,1)S(1)}, bf16[256,768]{1,0:T(8,128)(2,1)S(1)}, u32[]{:S(2)}, u32[]{:S(2)}) collective-permute-start(bf16[256,768]{1,0:T(8,128)(2,1)S(1)} %shard_map.39.own_ref), channel_id=1, source_target_pairs={{1,0},{0,1},{3,2},{2,3},{5,4},{4,5},{7,6},{6,7},{9,8},{8,9},{11,10... | collective-permute-start | bytes 1179656 | tf_op jit(solution)/shard_map/ppermute | solution.py:277

commit v3 on v0

v3 whole, which is shorter than its diff:
```python
import functools

import jax
import jax.numpy as jnp
from jax import lax
from jax.experimental import pallas as pl
from jax.experimental.pallas import tpu as pltpu
from jax.sharding import PartitionSpec as P

CAP = 8
SHARED = 2
KEPT = CAP - SHARED
SPLIT = KEPT // 2
LANES = 128
VMEM_LIMIT = 48 * 1024 * 1024
HIGHEST = lax.Precision.HIGHEST


def place(dest, members):
    owner = dest // CAP
    group = owner // members
    member = owner % members
    column = dest % CAP
    shared = member * SHARED + column
    index = column - SHARED
    third = member % 3
    halved = third == 2
    spread = column < SHARED
    core = jnp.where(
        spread, shared // CAP, jnp.where(halved, index // SPLIT, third)
    )
    chip = jnp.where(spread, 0, 1 + member // 3)
    row = jnp.where(
        spread, shared % CAP, jnp.where(halved, index % SPLIT, index + SPLIT)
    )
    return group * members + 2 * chip + core, row


def params():
    return pltpu.CompilerParams(vmem_limit_bytes=VMEM_LIMIT)


def iota(shape, axis):
    return lax.broadcasted_iota(jnp.int32, shape, axis)


def dot(a, b):
    return jnp.dot(a, b, preferred_element_type=jnp.float32)


def dot_t(a, b):
    return lax.dot_general(a, b, (((1,), (1,)), ((), ())), preferred_element_type=jnp.float32)


def ones_where(mask):
    return jnp.where(mask, 1.0, 0.0).astype(jnp.bfloat16)


def pack_kernel(members, embeds_ref, packed_ref, out_ref, unit_ref, last_ref):
    rows, width = embeds_ref.shape
    slots = out_ref.shape[0]
    devices = slots // CAP
    packed = packed_ref[...]
    label = (packed // slots).astype(jnp.float32)
    device, row = place(packed % slots, members)
    slot = jnp.where(row < CAP, device * CAP + row, -1)

    values = embeds_ref[...].astype(jnp.float32)
    total = jnp.sum(values * values, axis=1, keepdims=True)
    unit_ref[...] = (values * lax.rsqrt(total + 1e-06)).astype(jnp.bfloat16)

    here = iota((devices, rows), 0) == device
    ninth = dot(ones_where(here & (row == CAP)), unit_ref[...])
    for piece in range(width // LANES):
        last_ref[pl.ds(piece, devices, stride=CAP), :] = ninth[
            :, piece * LANES : (piece + 1) * LANES
        ]
    marks = jnp.where(iota((LANES, rows), 0) == row, label, 0.0).astype(jnp.bfloat16)
    labels = dot_t(ones_where(here), marks)
    for piece in range(width // LANES, CAP):
        last_ref[pl.ds(piece, devices, stride=CAP), :] = labels
    out_ref[:, width:] = last_ref[...].astype(jnp.bfloat16)

    block = 256
    for b in range(slots // block):
        pick = ones_where(b * block + iota((block, rows), 0) == slot)
        out_ref[b * block : (b + 1) * block, :width] = dot(pick, unit_ref[...]).astype(
            jnp.bfloat16
        )


def pack(embeds, cluster, dest, slots, members):
    rows, width = embeds.shape
    packed = (dest + slots * (cluster + 1)).reshape(1, rows)
    return pl.pallas_call(
        functools.partial(pack_kernel, members),
        out_shape=jax.ShapeDtypeStruct((slots, width + LANES), jnp.bfloat16),
        scratch_shapes=[
            pltpu.VMEM((rows, width), jnp.bfloat16),
            pltpu.VMEM((slots, LANES), jnp.float32),
        ],
        compiler_params=params(),
    )(embeds, packed)


def spread_labels(labels, slots):
    row = iota((slots, LANES), 0)
    lane = iota((slots, LANES), 1)
    repeat = ones_where(row // CAP == lane)
    return jnp.where(lane == row % CAP, dot(repeat, labels.astype(jnp.bfloat16)), 0.0).astype(
        jnp.bfloat16
    )


def fold_block(best, keys, queries, key_labels, query_labels, skip=None):
    same = key_labels == query_labels
    if skip is not None:
        same = same & ~skip
    return jnp.maximum(
        best, jnp.max(jnp.where(same, dot_t(keys, queries), -1.0), axis=0, keepdims=True)
    )


def own_kernel(rows_ref, best_ref, labels_ref, last_ref, ninth_ref, column_ref):
    slots, wide = rows_ref.shape
    width = wide - LANES
    sources = slots // CAP
    last_ref[...] = rows_ref[:, width:].astype(jnp.float32)
    for piece in range(width // LANES):
        ninth_ref[:, piece * LANES : (piece + 1) * LANES] = last_ref[
            pl.ds(piece, sources, stride=CAP), :
        ].astype(jnp.bfloat16)
    labels = last_ref[pl.ds(width // LANES, sources, stride=CAP), :]
    spots = spread_labels(labels, slots)
    ones = jnp.ones((LANES, LANES), jnp.bfloat16)
    column_ref[:slots, :] = dot(spots, ones)
    at_ninth = ones_where(iota((LANES, LANES), 0) == CAP)
    column_ref[slots:, :] = dot(labels.astype(jnp.bfloat16), at_ninth)
    at_ninth = ones_where(iota((CAP, LANES), 1) == CAP)
    row_labels = jnp.concatenate(
        [dot_t(ones[:CAP], spots), dot_t(at_ninth, labels.astype(jnp.bfloat16))], axis=1
    )
    labels_ref[...] = row_labels

    block = 256
    starts = list(range(0, slots, block)) + [slots]
    sizes = [block] * (slots // block) + [sources]

    def read(i):
        if starts[i] == slots:
            return ninth_ref[...]
        return rows_ref[starts[i] : starts[i] + block, :width]

    for q, (query, size) in enumerate(zip(starts, sizes)):
        best = jnp.full((1, size), -1.0, jnp.float32)
        queries = read(q)
        for k, (key, count) in enumerate(zip(starts, sizes)):
            skip = None
            if k == q:
                skip = iota((count, size), 0) == iota((count, size), 1)
            best = fold_block(
                best,
                read(k),
                queries,
                column_ref[key : key + count, :1],
                row_labels[:1, query : query + size],
                skip,
            )
        best_ref[:, query : query + size] = best


def own_best(arrived):
    slots, wide = arrived.shape
    count = slots + slots // CAP
    return pl.pallas_call(
        own_kernel,
        out_shape=(
            jax.ShapeDtypeStruct((1, count), jnp.float32),
            jax.ShapeDtypeStruct((CAP, count), jnp.float32),
        ),
        scratch_shapes=[
            pltpu.VMEM((slots, LANES), jnp.float32),
            pltpu.VMEM((slots // CAP, wide - LANES), jnp.bfloat16),
            pltpu.VMEM((count, LANES), jnp.float32),
        ],
        compiler_params=params(),
    )(arrived)


def cross_kernel(best_ref, labels_ref, rows_ref, other_ref, out_ref, last_ref, column_ref):
    slots, wide = rows_ref.shape
    width = wide - LANES
    sources = slots // CAP
    last_ref[...] = other_ref[:, width:].astype(jnp.float32)
    labels = last_ref[pl.ds(width // LANES, sources, stride=CAP), :]
    column_ref[...] = dot(
        spread_labels(labels, slots), jnp.ones((LANES, LANES), jnp.bfloat16)
    )
    block = 256
    results = []
    for q in range(0, slots, block):
        best = best_ref[:, q : q + block]
        for k in range(0, slots, block):
            best = fold_block(
                best,
                other_ref[k : k + block, :width],
                rows_ref[q : q + block, :width],
                column_ref[k : k + block, :1],
                labels_ref[:1, q : q + block],
            )
        results.append(best)
    local = jnp.concatenate(results, axis=1)

    per = LANES // CAP
    source = iota((sources, LANES), 0)
    lane = iota((sources, LANES), 1)
    spots = jnp.concatenate(
        [
            jnp.broadcast_to(local[:, t * LANES : (t + 1) * LANES], (per, LANES))
            for t in range(sources // per)
        ],
        axis=0,
    )
    ninth = jnp.broadcast_to(best_ref[:, slots:], (sources, LANES))
    mine = jnp.concatenate(
        [
            jnp.where(lane // CAP == source % per, spots, 0.0),
            jnp.where(lane == source, ninth, 0.0),
        ],
        axis=1,
    )
    fold = jnp.concatenate(
        [
            jnp.where(iota((LANES, LANES), 0) % CAP == iota((LANES, LANES), 1), 1.0, 0.0),
            jnp.where(iota((LANES, LANES), 1) == CAP, 1.0, 0.0),
        ],
        axis=0,
    )
    out_ref[...] = jnp.dot(
        mine, fold, precision=HIGHEST, preferred_element_type=jnp.float32
    )


def cross_best(best, labels, arrived, other):
    slots = arrived.shape[0]
    return pl.pallas_call(
        cross_kernel,
        out_shape=jax.ShapeDtypeStruct((slots // CAP, LANES), jnp.float32),
        scratch_shapes=[
            pltpu.VMEM((slots, LANES), jnp.float32),
            pltpu.VMEM((slots, LANES), jnp.float32),
        ],
        compiler_params=params(),
    )(best, labels, arrived, other)


def lookup_kernel(members, table_ref, dest_ref, out_ref):
    devices = table_ref.shape[0]
    rows = dest_ref.shape[1]
    device, row = place(dest_ref[...], members)
    pick = jnp.where(iota((devices, rows), 0) == device, 1.0, 0.0)
    found = lax.dot_general(
        table_ref[...], pick, (((0,), (0,)), ((), ())), precision=HIGHEST,
        preferred_element_type=jnp.float32,
    )
    out_ref[...] = jnp.max(
        jnp.where(iota((LANES, rows), 0) == row, found, -1.0), axis=0, keepdims=True
    )


def lookup(table, dest, members):
    rows = dest.shape[0]
    return pl.pallas_call(
        functools.partial(lookup_kernel, members),
        out_shape=jax.ShapeDtypeStruct((1, rows), jnp.float32),
        compiler_params=params(),
    )(table, dest.reshape(1, rows)).reshape(rows)


def shards(embeds, cluster, dest):
    members = lax.axis_size("mem")
    devices = lax.axis_size("grp") * members
    width = embeds.shape[1]
    slots = devices * CAP
    outgoing = pack(embeds, cluster, dest, slots, members)
    arrived = lax.all_to_all(
        outgoing.reshape(devices, CAP, width + LANES),
        ("grp", "mem"),
        split_axis=0,
        concat_axis=0,
        tiled=True,
    ).reshape(slots, width + LANES)
    other = lax.ppermute(arrived, "mem", [(m, m ^ 1) for m in range(members)])
    best, labels = own_best(arrived)
    table = cross_best(best, labels, arrived, other)
    returned = lax.all_to_all(
        table.reshape(devices, 1, LANES),
        ("grp", "mem"),
        split_axis=0,
        concat_axis=0,
        tiled=True,
    ).reshape(devices, LANES)
    return lookup(returned, dest, members)


def solution(mesh):
    placed = (P(("grp", "mem"), None), P(("grp", "mem")), P(("grp", "mem")))
    return jax.shard_map(
        shards, mesh=mesh, in_specs=placed, out_specs=P(("grp", "mem")), check_vma=False
    )
```

time: 162 us -> 63.3 us (0.39)
  waiting for transfers between devices: 53 us -> 0.14 us
  matrix products: 18.7 us -> 0 us
  between operations: 13.5 us -> 0.02 us
  starting transfers between devices: 12.4 us -> 0.87 us
  local copies, waits for them, and re-layouts: 9.33 us -> 1.14 us
  Pallas kernels: 0 us -> 8.07 us
  other arithmetic: 6.75 us -> 0.7 us
  blocking collectives: 48.4 us -> 52.1 us
    all_gather x1 -> x0, waiting for transfers between devices: 33.6 us -> none  [shards(): lax.all_gather(local, 'mem', axis=0, tiled=True)]
    all_to_all x2 -> x0, waiting for transfers between devices: 19.4 us -> none  [the longest x1 9.87 us: shards(): lax.all_to_all(out_labels.reshape(devices, capacity), ('grp', 'mem'), spl...]
    dot_general x1 -> x0, matrix products: 18.7 us -> none  [fold_with(): lax.dot_general(queries, columns, (((1,), (1,)), ((), ())), preferred_ele...]
    all_to_all x1 -> x2, blocking collectives: 36.3 us -> 52.1 us  [the longest x1 39.1 us: shards(): lax.all_to_all(outgoing.reshape(devices, CAP, width + LANES), ('grp', 'me...]
    all_to_all x2 -> x0, starting transfers between devices: 12.4 us -> none  [the longest x1 8.13 us: shards(): lax.all_to_all(results.reshape(devices, capacity), ('grp', 'mem'), split_...]
    all_gather x1 -> x0, blocking collectives: 12.1 us -> none  [shards(): lax.all_gather(local_labels, 'mem', axis=0, tiled=True)]
    pallas_call x0 -> x4, Pallas kernels: none -> 8.07 us  [the longest x1 3.27 us: own_best(): pl.pallas_call(own_kernel, out_shape=(jax.ShapeDtypeStruct((1, count), jn...]
    scatter x1 -> x0, local copies, waits for them, and re-layouts: 3.77 us -> none  [shards(): out_labels = jnp.full((slots,), -1.0, jnp.bfloat16).at[dest].set(labels)]
  transfers between devices with their start and end apart: 3 -> 1, of which waited for: 3 -> 1; matrix products, arithmetic and copies ran while one was open for 3% -> 0% of each run, Pallas kernels for 0% -> 5%
where the time goes in v3:
time: 63.3 us; the launch traced here: 63.1 us
  blocking collectives  52.1 us (82%)
  Pallas kernels  8.07 us (13%)
  local copies, waits for them, and re-layouts  1.14 us (2%)
  starting transfers between devices  0.87 us (1%)
  other arithmetic  0.7 us (1%)
    all_to_all x1, blocking collectives, shards(): lax.all_to_all(outgoing.reshape(devices, CAP, width + LANES), ('grp', 'me...  39.1 us
    all_to_all x1, blocking collectives, shards(): lax.all_to_all(table.reshape(devices, 1, LANES), ('grp', 'mem'), split_ax...  13.1 us
    pallas_call x1, Pallas kernels, own_best(): pl.pallas_call(own_kernel, out_shape=(jax.ShapeDtypeStruct((1, count), jn...  3.27 us
    pallas_call x1, Pallas kernels, cross_best(): pl.pallas_call(cross_kernel, out_shape=jax.ShapeDtypeStruct((slots // CAP...  2.4 us
    pallas_call x1, Pallas kernels, pack(): pl.pallas_call(functools.partial(pack_kernel, members), out_shape=jax.Sha...  1.38 us
  transfers between devices with their start and end apart: 1, of which 1 were waited for; matrix products, arithmetic and copies ran while one was open for 0% of the time, Pallas kernels for 5%

profile of v3, /device:TPU:1, one launch (start us, length us, event | category | flops | bytes accessed | tf_op | source)
XLA Modules:
  0.0 63.1 jit_solution(18350528413438935319)
XLA Ops:
  0.0 0.7 %multiply_add_fusion = s32[512]{0:T(512)S(1)} fusion(s32[512]{0:T(512)} %param.5, s32[512]{0:T(512)} %param.4), kind=kLoop, calls=%fused_computation | loop fusion | flops 1536 | bytes 6144 | tf_op jit(solution)/shard_map/add | solution.py:94
  0.7 0.0 copy-start
  0.7 1.1 %copy-done = bf16[512,768]{1,0:T(8,128)(2,1)S(1)} copy-done((bf16[512,768]{1,0:T(8,128)(2,1)S(1)}, bf16[512,768]{1,0:T(8,128)(2,1)}, u32[]{:S(2)}) %copy-start) | copy-done | bytes 786456
  1.8 1.4 %shard_map.37 = bf16[1024,896]{1,0:T(8,128)(2,1)S(1)} custom-call(bf16[512,768]{1,0:T(8,128)(2,1)S(1)} %copy-done, s32[1,512]{1,0:T(1,128)S(1)} %bitcast.16), custom_call_target="tpu_custom_call" | custom-call | tf_op jit(solution)/shard_map/pallas_call | solution.py:95
  3.2 39.1 %all_to_all.10 = bf16[128,8,896]{2,1,0:T(8,128)(2,1)S(1)} all-to-all(bf16[128,8,896]{2,1,0:T(8,128)(2,1)S(1)} %bitcast.12), channel_id=1, replica_groups=mesh['grp'=16,'mem'=8] {'grp','mem'}, dimensions={0} | all-to-all | bytes 3670016 | tf_op jit(solution)/shard_map/all_to_all | solution.py:286
  42.3 0.9 %collective-permute-start = (bf16[1024,896]{1,0:T(8,128)(2,1)S(1)}, bf16[1024,896]{1,0:T(8,128)(2,1)S(1)}, u32[]{:S(2)}, u32[]{:S(2)}) collective-permute-start(bf16[1024,896]{1,0:T(8,128)(2,1)S(1)} %bitcast.9), channel_id=1, source_target_pairs={{0,1},{1,0},{2,3},{3,2},{4,5},{5,4},{6,7},{7,6},{8,9},{9,8},{10,11... | collective-permute-start | bytes 5505032 | tf_op jit(solution)/shard_map/ppermute | solution.py:293
  43.2 3.3 %shard_map.38 = (f32[1,1152]{1,0:T(1,128)S(1)}, f32[8,1152]{1,0:T(8,128)S(1)}) custom-call(bf16[1024,896]{1,0:T(8,128)(2,1)S(1)} %bitcast.10), custom_call_target="tpu_custom_call" | custom-call | tf_op jit(solution)/shard_map/pallas_call | solution.py:175
  46.4 0.1 collective-permute-done.other_ref
  46.6 0.0 copy-start.1
  46.6 2.4 %shard_map.39 = f32[128,128]{1,0:T(8,128)S(1)} custom-call(f32[1,1152]{1,0:T(1,128)S(1)} %get-tuple-element.7.best_ref, f32[8,1152]{1,0:T(8,128)S(1)} %get-tuple-element.8.labels_ref, bf16[1024,896]{1,0:T(8,128)(2,1)S(1)} %bitcast.11, bf16[1024,896]{1,0:T(8,128)(2,1)S(1)} %collective-permute-done.other_ref), custom_call_target="tpu_custom_call" | custom-call | tf_op jit(solution)/shard_map/pallas_call | solution.py:246
  49.0 13.1 %all_to_all.11 = f32[128,1,128]{2,1,0:T(1,128)S(1)} all-to-all(f32[128,1,128]{2,1,0:T(1,128)S(1)} %bitcast.13), channel_id=1, replica_groups=mesh['grp'=16,'mem'=8] {'grp','mem'}, dimensions={0} | all-to-all | bytes 131072 | tf_op jit(solution)/shard_map/all_to_all | solution.py:296
  62.0 0.0 copy-done.1
  62.0 1.0 %shard_map.40 = f32[1,512]{1,0:T(1,128)} custom-call(f32[128,128]{1,0:T(8,128)S(1)} %bitcast.14, s32[1,512]{1,0:T(1,128)S(1)} %bitcast.15), custom_call_target="tpu_custom_call" | custom-call | tf_op jit(solution)/shard_map/pallas_call | solution.py:273
Async XLA Ops:
  0.7 1.1 %copy-start = (bf16[512,768]{1,0:T(8,128)(2,1)S(1)}, bf16[512,768]{1,0:T(8,128)(2,1)}, u32[]{:S(2)}) copy-start(bf16[512,768]{1,0:T(8,128)(2,1)} %embeds_ref.1) | copy-start | bytes 2359300
  42.3 4.3 %collective-permute-start = (bf16[1024,896]{1,0:T(8,128)(2,1)S(1)}, bf16[1024,896]{1,0:T(8,128)(2,1)S(1)}, u32[]{:S(2)}, u32[]{:S(2)}) collective-permute-start(bf16[1024,896]{1,0:T(8,128)(2,1)S(1)} %bitcast.9), channel_id=1, source_target_pairs={{0,1},{1,0},{2,3},{3,2},{4,5},{5,4},{6,7},{7,6},{8,9},{9,8},{10,11... | collective-permute-start | bytes 5505032 | tf_op jit(solution)/shard_map/ppermute | solution.py:293
  46.6 15.5 %copy-start.1 = (s32[512]{0:T(512)S(1)}, s32[512]{0:T(512)}, u32[]{:S(2)}) copy-start(s32[512]{0:T(512)} %param.5) | copy-start | bytes 6148

commit v4 on v3

--- a/solution.py
+++ b/solution.py
@@ -103,11 +103,16 @@
     )(embeds, packed)
 
 
+def ninth_lane(source):
+    windows = LANES // CAP
+    return CAP * ((source + 1) % windows) + source // windows
+
+
 def spread_labels(labels, slots):
     row = iota((slots, LANES), 0)
     lane = iota((slots, LANES), 1)
     repeat = ones_where(row // CAP == lane)
-    return jnp.where(lane == row % CAP, dot(repeat, labels.astype(jnp.bfloat16)), 0.0).astype(
+    return jnp.where(lane == row % CAP, dot(repeat, labels), 0.0).astype(
         jnp.bfloat16
     )
 
@@ -130,15 +135,18 @@
         ninth_ref[:, piece * LANES : (piece + 1) * LANES] = last_ref[
             pl.ds(piece, sources, stride=CAP), :
         ].astype(jnp.bfloat16)
-    labels = last_ref[pl.ds(width // LANES, sources, stride=CAP), :]
+    labels = last_ref[pl.ds(width // LANES, sources, stride=CAP), :].astype(jnp.bfloat16)
     spots = spread_labels(labels, slots)
+    order = ones_where(iota((sources, LANES), 0) == ninth_lane(iota((sources, LANES), 1)))
+    ninth_ref[...] = dot(order, ninth_ref[...]).astype(jnp.bfloat16)
+    labels = dot(order, labels).astype(jnp.bfloat16)
     ones = jnp.ones((LANES, LANES), jnp.bfloat16)
     column_ref[:slots, :] = dot(spots, ones)
     at_ninth = ones_where(iota((LANES, LANES), 0) == CAP)
-    column_ref[slots:, :] = dot(labels.astype(jnp.bfloat16), at_ninth)
+    column_ref[slots:, :] = dot(labels, at_ninth)
     at_ninth = ones_where(iota((CAP, LANES), 1) == CAP)
     row_labels = jnp.concatenate(
-        [dot_t(ones[:CAP], spots), dot_t(at_ninth, labels.astype(jnp.bfloat16))], axis=1
+        [dot_t(ones[:CAP], spots), dot_t(at_ninth, labels)], axis=1
     )
     labels_ref[...] = row_labels
 
@@ -192,53 +200,62 @@
     width = wide - LANES
     sources = slots // CAP
     last_ref[...] = other_ref[:, width:].astype(jnp.float32)
-    labels = last_ref[pl.ds(width // LANES, sources, stride=CAP), :]
+    labels = last_ref[pl.ds(width // LANES, sources, stride=CAP), :].astype(jnp.bfloat16)
     column_ref[...] = dot(
         spread_labels(labels, slots), jnp.ones((LANES, LANES), jnp.bfloat16)
     )
     block = 256
-    results = []
-    for q in range(0, slots, block):
-        best = best_ref[:, q : q + block]
-        for k in range(0, slots, block):
-            best = fold_block(
-                best,
-                other_ref[k : k + block, :width],
-                rows_ref[q : q + block, :width],
-                column_ref[k : k + block, :1],
-                labels_ref[:1, q : q + block],
-            )
-        results.append(best)
-    local = jnp.concatenate(results, axis=1)
-
-    per = LANES // CAP
-    source = iota((sources, LANES), 0)
-    lane = iota((sources, LANES), 1)
-    spots = jnp.concatenate(
-        [
-            jnp.broadcast_to(local[:, t * LANES : (t + 1) * LANES], (per, LANES))
-            for t in range(sources // per)
-        ],
-        axis=0,
-    )
-    ninth = jnp.broadcast_to(best_ref[:, slots:], (sources, LANES))
-    mine = jnp.concatenate(
-        [
-            jnp.where(lane // CAP == source % per, spots, 0.0),
-            jnp.where(lane == source, ninth, 0.0),
-        ],
-        axis=1,
-    )
-    fold = jnp.concatenate(
-        [
-            jnp.where(iota((LANES, LANES), 0) % CAP == iota((LANES, LANES), 1), 1.0, 0.0),
-            jnp.where(iota((LANES, LANES), 1) == CAP, 1.0, 0.0),
-        ],
-        axis=0,
-    )
-    out_ref[...] = jnp.dot(
-        mine, fold, precision=HIGHEST, preferred_element_type=jnp.float32
-    )
+
+    def run(last_key, first_query):
+        own = [best_ref[:, q : q + block] for q in range(0, slots, block)]
+        gained = [jnp.full((1, LANES), -1.0, jnp.float32)] * (slots // LANES)
+        for k in range(0, last_key, block):
+            widest = jnp.full((block, LANES), -1.0, jnp.float32)
+            for q in range(first_query, slots, block):
+                scores = dot_t(other_ref[k : k + block, :width], rows_ref[q : q + block, :width])
+                same = column_ref[k : k + block, :1] == labels_ref[:1, q : q + block]
+                scores = jnp.where(same, scores, -1.0)
+                own[q // block] = jnp.maximum(
+                    own[q // block], jnp.max(scores, axis=0, keepdims=True)
+                )
+                for lane in range(0, block, LANES):
+                    widest = jnp.maximum(widest, scores[:, lane : lane + LANES])
+            for j in range(0, block, LANES):
+                gained[(k + j) // LANES] = jnp.max(
+                    widest[j : j + LANES].T, axis=0, keepdims=True
+                )
+        windows = LANES // CAP
+        own = jnp.concatenate(own, axis=1)
+        tiles = range(slots // LANES)
+        own = jnp.concatenate(
+            [
+                jnp.broadcast_to(own[:, t * LANES : (t + 1) * LANES], (windows, LANES))
+                for t in tiles
+            ],
+            axis=0,
+        )
+        gained = jnp.concatenate(
+            [jnp.broadcast_to(gained[t], (windows, LANES)) for t in tiles], axis=0
+        )
+        gained = pltpu.roll(gained, LANES // 2, 1)
+        ninth = jnp.broadcast_to(best_ref[:, slots:], (sources, LANES))
+        window = iota((sources, LANES), 1) // CAP
+        mine = iota((sources, LANES), 0) % windows
+        out_ref[...] = jnp.where(
+            window == mine,
+            own,
+            jnp.where(window == (mine + windows // 2) % windows, gained, ninth),
+        )
+
+    core = lax.axis_index("mem") % 2
+
+    @pl.when(core == 0)
+    def _():
+        run(slots // 2, 0)
+
+    @pl.when(core == 1)
+    def _():
+        run(slots, slots // 2)
 
 
 def cross_best(best, labels, arrived, other):
@@ -257,14 +274,24 @@
 def lookup_kernel(members, table_ref, dest_ref, out_ref):
     devices = table_ref.shape[0]
     rows = dest_ref.shape[1]
+    windows = LANES // CAP
+    me = lax.axis_index("grp") * members + lax.axis_index("mem")
+    mine = me % windows
+    table = table_ref[...]
+    turned = pltpu.roll(table, LANES // 2, 1)
+    even = iota((devices, LANES), 0) % 2 == 0
+    other = jnp.where(even, pltpu.roll(turned, devices - 1, 0), pltpu.roll(turned, 1, 0))
+    window = iota((devices, LANES), 1) // CAP
+    table = jnp.where(window == mine, jnp.maximum(table, other), table)
     device, row = place(dest_ref[...], members)
     pick = jnp.where(iota((devices, rows), 0) == device, 1.0, 0.0)
     found = lax.dot_general(
-        table_ref[...], pick, (((0,), (0,)), ((), ())), precision=HIGHEST,
+        table, pick, (((0,), (0,)), ((), ())), precision=HIGHEST,
         preferred_element_type=jnp.float32,
     )
+    lane = jnp.where(row < CAP, CAP * mine + row, ninth_lane(me))
     out_ref[...] = jnp.max(
-        jnp.where(iota((LANES, rows), 0) == row, found, -1.0), axis=0, keepdims=True
+        jnp.where(iota((LANES, rows), 0) == lane, found, -1.0), axis=0, keepdims=True
     )
 
 

time: 63.3 us -> 62.6 us (0.989)
  Pallas kernels: 8.07 us -> 7.35 us
    pallas_call x1, Pallas kernels: 2.4 us -> 1.64 us  [cross_best(): pl.pallas_call(cross_kernel, out_shape=jax.ShapeDtypeStruct((slots // CAP...]
where the time goes in v4:
time: 62.6 us; the launch traced here: 62.3 us
  blocking collectives  52.1 us (83%)
  Pallas kernels  7.35 us (12%)
  local copies, waits for them, and re-layouts  1.14 us (2%)
  starting transfers between devices  0.87 us (1%)
  other arithmetic  0.7 us (1%)
    all_to_all x1, blocking collectives, shards(): lax.all_to_all(outgoing.reshape(devices, CAP, width + LANES), ('grp', 'me...  39.1 us
    all_to_all x1, blocking collectives, shards(): lax.all_to_all(table.reshape(devices, 1, LANES), ('grp', 'mem'), split_ax...  13 us
    pallas_call x1, Pallas kernels, own_best(): pl.pallas_call(own_kernel, out_shape=(jax.ShapeDtypeStruct((1, count), jn...  3.25 us
    pallas_call x1, Pallas kernels, cross_best(): pl.pallas_call(cross_kernel, out_shape=jax.ShapeDtypeStruct((slots // CAP...  1.64 us
    pallas_call x1, Pallas kernels, pack(): pl.pallas_call(functools.partial(pack_kernel, members), out_shape=jax.Sha...  1.38 us
  transfers between devices with their start and end apart: 1, of which 1 were waited for; matrix products, arithmetic and copies ran while one was open for 0% of the time, Pallas kernels for 5%

profile of v4, /device:TPU:1, one launch (start us, length us, event | category | flops | bytes accessed | tf_op | source)
XLA Modules:
  0.0 62.3 jit_solution(6694415227236372984)
XLA Ops:
  0.0 0.7 %multiply_add_fusion = s32[512]{0:T(512)S(1)} fusion(s32[512]{0:T(512)} %param.5, s32[512]{0:T(512)} %param.4), kind=kLoop, calls=%fused_computation | loop fusion | flops 1536 | bytes 6144 | tf_op jit(solution)/shard_map/add | solution.py:94
  0.7 0.0 copy-start
  0.7 1.1 %copy-done = bf16[512,768]{1,0:T(8,128)(2,1)S(1)} copy-done((bf16[512,768]{1,0:T(8,128)(2,1)S(1)}, bf16[512,768]{1,0:T(8,128)(2,1)}, u32[]{:S(2)}) %copy-start) | copy-done | bytes 786456
  1.8 1.4 %shard_map.37 = bf16[1024,896]{1,0:T(8,128)(2,1)S(1)} custom-call(bf16[512,768]{1,0:T(8,128)(2,1)S(1)} %copy-done, s32[1,512]{1,0:T(1,128)S(1)} %bitcast.16), custom_call_target="tpu_custom_call" | custom-call | tf_op jit(solution)/shard_map/pallas_call | solution.py:95
  3.2 39.1 %all_to_all.10 = bf16[128,8,896]{2,1,0:T(8,128)(2,1)S(1)} all-to-all(bf16[128,8,896]{2,1,0:T(8,128)(2,1)S(1)} %bitcast.12), channel_id=1, replica_groups=mesh['grp'=16,'mem'=8] {'grp','mem'}, dimensions={0} | all-to-all | bytes 3670016 | tf_op jit(solution)/shard_map/all_to_all | solution.py:313
  42.3 0.9 %collective-permute-start = (bf16[1024,896]{1,0:T(8,128)(2,1)S(1)}, bf16[1024,896]{1,0:T(8,128)(2,1)S(1)}, u32[]{:S(2)}, u32[]{:S(2)}) collective-permute-start(bf16[1024,896]{1,0:T(8,128)(2,1)S(1)} %bitcast.9), channel_id=1, source_target_pairs={{0,1},{1,0},{2,3},{3,2},{4,5},{5,4},{6,7},{7,6},{8,9},{9,8},{10,11... | collective-permute-start | bytes 5505032 | tf_op jit(solution)/shard_map/ppermute | solution.py:320
  43.2 3.2 %shard_map.38 = (f32[1,1152]{1,0:T(1,128)S(1)}, f32[8,1152]{1,0:T(8,128)S(1)}) custom-call(bf16[1024,896]{1,0:T(8,128)(2,1)S(1)} %bitcast.10), custom_call_target="tpu_custom_call" | custom-call | tf_op jit(solution)/shard_map/pallas_call | solution.py:183
  46.4 0.2 collective-permute-done.other_ref
  46.6 0.0 copy-start.1
  46.6 1.6 %shard_map.39 = f32[128,128]{1,0:T(8,128)S(1)} custom-call(f32[1,1152]{1,0:T(1,128)S(1)} %get-tuple-element.7.best_ref, f32[8,1152]{1,0:T(8,128)S(1)} %get-tuple-element.8.labels_ref, bf16[1024,896]{1,0:T(8,128)(2,1)S(1)} %bitcast.11, bf16[1024,896]{1,0:T(8,128)(2,1)S(1)} %collective-permute-done.other_ref), custom_call_target="tpu_custom_call" | custom-call | tf_op jit(solution)/shard_map/pallas_call | solution.py:263
  48.2 13.0 %all_to_all.11 = f32[128,1,128]{2,1,0:T(1,128)S(1)} all-to-all(f32[128,1,128]{2,1,0:T(1,128)S(1)} %bitcast.13), channel_id=1, replica_groups=mesh['grp'=16,'mem'=8] {'grp','mem'}, dimensions={0} | all-to-all | bytes 131072 | tf_op jit(solution)/shard_map/all_to_all | solution.py:323
  61.3 0.0 copy-done.1
  61.3 1.1 %shard_map.40 = f32[1,512]{1,0:T(1,128)} custom-call(f32[128,128]{1,0:T(8,128)S(1)} %bitcast.14, s32[1,512]{1,0:T(1,128)S(1)} %bitcast.15), custom_call_target="tpu_custom_call" | custom-call | tf_op jit(solution)/shard_map/pallas_call | solution.py:300
Async XLA Ops:
  0.7 1.1 %copy-start = (bf16[512,768]{1,0:T(8,128)(2,1)S(1)}, bf16[512,768]{1,0:T(8,128)(2,1)}, u32[]{:S(2)}) copy-start(bf16[512,768]{1,0:T(8,128)(2,1)} %embeds_ref.1) | copy-start | bytes 2359300
  42.3 4.3 %collective-permute-start = (bf16[1024,896]{1,0:T(8,128)(2,1)S(1)}, bf16[1024,896]{1,0:T(8,128)(2,1)S(1)}, u32[]{:S(2)}, u32[]{:S(2)}) collective-permute-start(bf16[1024,896]{1,0:T(8,128)(2,1)S(1)} %bitcast.9), channel_id=1, source_target_pairs={{0,1},{1,0},{2,3},{3,2},{4,5},{5,4},{6,7},{7,6},{8,9},{9,8},{10,11... | collective-permute-start | bytes 5505032 | tf_op jit(solution)/shard_map/ppermute | solution.py:320
  46.6 14.7 %copy-start.1 = (s32[512]{0:T(512)S(1)}, s32[512]{0:T(512)}, u32[]{:S(2)}) copy-start(s32[512]{0:T(512)} %param.5) | copy-start | bytes 6148

commit v5 on v4

--- a/solution.py
+++ b/solution.py
@@ -56,51 +56,55 @@
     return jnp.where(mask, 1.0, 0.0).astype(jnp.bfloat16)
 
 
-def pack_kernel(members, embeds_ref, packed_ref, out_ref, unit_ref, last_ref):
+def pack_kernel(embeds_ref, packed_ref, pick_ref, out_ref, unit_ref, last_ref):
     rows, width = embeds_ref.shape
     slots = out_ref.shape[0]
     devices = slots // CAP
     packed = packed_ref[...]
-    label = (packed // slots).astype(jnp.float32)
-    device, row = place(packed % slots, members)
-    slot = jnp.where(row < CAP, device * CAP + row, -1)
+    spot = packed % (2 * slots)
+    label = (packed // (2 * slots)).astype(jnp.float32)
+    device = jnp.where(spot < slots, spot // CAP, spot - slots)
+    row = jnp.where(spot < slots, spot % CAP, CAP)
 
     values = embeds_ref[...].astype(jnp.float32)
     total = jnp.sum(values * values, axis=1, keepdims=True)
     unit_ref[...] = (values * lax.rsqrt(total + 1e-06)).astype(jnp.bfloat16)
 
-    here = iota((devices, rows), 0) == device
-    ninth = dot(ones_where(here & (row == CAP)), unit_ref[...])
+    ninth = dot(pick_ref[slots:, :].astype(jnp.bfloat16), unit_ref[...])
     for piece in range(width // LANES):
         last_ref[pl.ds(piece, devices, stride=CAP), :] = ninth[
             :, piece * LANES : (piece + 1) * LANES
         ]
+    here = ones_where(iota((devices, rows), 0) == device)
     marks = jnp.where(iota((LANES, rows), 0) == row, label, 0.0).astype(jnp.bfloat16)
-    labels = dot_t(ones_where(here), marks)
+    labels = dot_t(here, marks)
     for piece in range(width // LANES, CAP):
         last_ref[pl.ds(piece, devices, stride=CAP), :] = labels
     out_ref[:, width:] = last_ref[...].astype(jnp.bfloat16)
 
     block = 256
-    for b in range(slots // block):
-        pick = ones_where(b * block + iota((block, rows), 0) == slot)
-        out_ref[b * block : (b + 1) * block, :width] = dot(pick, unit_ref[...]).astype(
+    for b in range(0, slots, block):
+        out_ref[b : b + block, :width] = dot(pick_ref[b : b + block, :].astype(jnp.bfloat16), unit_ref[...]).astype(
             jnp.bfloat16
         )
 
 
 def pack(embeds, cluster, dest, slots, members):
     rows, width = embeds.shape
-    packed = (dest + slots * (cluster + 1)).reshape(1, rows)
+    devices = slots // CAP
+    device, row = place(dest, members)
+    spot = jnp.where(row < CAP, device * CAP + row, slots + device)
+    packed = (spot + 2 * slots * (cluster + 1)).reshape(1, rows)
+    pick = jnp.where(iota((slots + devices, rows), 0) == spot[None], 1.0, 0.0)
     return pl.pallas_call(
-        functools.partial(pack_kernel, members),
+        pack_kernel,
         out_shape=jax.ShapeDtypeStruct((slots, width + LANES), jnp.bfloat16),
         scratch_shapes=[
             pltpu.VMEM((rows, width), jnp.bfloat16),
             pltpu.VMEM((slots, LANES), jnp.float32),
         ],
         compiler_params=params(),
-    )(embeds, packed)
+    )(embeds, packed, pick)
 
 
 def ninth_lane(source):

time: 62.6 us -> 61.9 us (0.989)
  local copies, waits for them, and re-layouts: 1.14 us -> 0.03 us
    unnamed x4, local copies, waits for them, and re-layouts: 1.14 us -> 0.03 us
where the time goes in v5:
time: 61.9 us; the launch traced here: 61.7 us
  blocking collectives  52.1 us (84%)
  Pallas kernels  7.38 us (12%)
  other arithmetic  1.13 us (2%)
  starting transfers between devices  0.87 us (1%)
    all_to_all x1, blocking collectives, shards(): lax.all_to_all(outgoing.reshape(devices, CAP, width + LANES), ('grp', 'me...  39.1 us
    all_to_all x1, blocking collectives, shards(): lax.all_to_all(table.reshape(devices, 1, LANES), ('grp', 'mem'), split_ax...  13 us
    pallas_call x1, Pallas kernels, own_best(): pl.pallas_call(own_kernel, out_shape=(jax.ShapeDtypeStruct((1, count), jn...  3.25 us
    pallas_call x1, Pallas kernels, cross_best(): pl.pallas_call(cross_kernel, out_shape=jax.ShapeDtypeStruct((slots // CAP...  1.64 us
    pallas_call x1, Pallas kernels, pack(): pl.pallas_call(pack_kernel, out_shape=jax.ShapeDtypeStruct((slots, width...  1.41 us
  transfers between devices with their start and end apart: 1, of which 1 were waited for; matrix products, arithmetic and copies ran while one was open for 0% of the time, Pallas kernels for 5%

profile of v5, /device:TPU:1, one launch (start us, length us, event | category | flops | bytes accessed | tf_op | source)
XLA Modules:
  0.0 61.7 jit_solution(15884939907297920762)
XLA Ops:
  0.0 0.0 copy-start
  0.0 0.8 %multiply_add_fusion = (s32[512]{0:T(512)S(1)}, s32[512]{0:T(512)S(1)}) fusion(s32[512]{0:T(512)} %param.4, s32[512]{0:T(512)} %param.5), kind=kLoop, calls=%fused_computation.28 | loop fusion | flops 53760 | bytes 8192 | tf_op jit(solution)/shard_map/add | solution.py:97
  0.8 0.3 fusion.pick_ref
  1.1 0.0 copy-done
  1.2 1.4 %shard_map.37 = bf16[1024,896]{1,0:T(8,128)(2,1)S(1)} custom-call(bf16[512,768]{1,0:T(8,128)(2,1)S(1)} %copy-done, s32[1,512]{1,0:T(1,128)S(1)} %bitcast.15, f32[1152,512]{1,0:T(8,128)S(1)} %fusion.pick_ref), custom_call_target="tpu_custom_call" | custom-call | tf_op jit(solution)/shard_map/pallas_call | solution.py:99
  2.6 39.1 %all_to_all.10 = bf16[128,8,896]{2,1,0:T(8,128)(2,1)S(1)} all-to-all(bf16[128,8,896]{2,1,0:T(8,128)(2,1)S(1)} %bitcast.12), channel_id=1, replica_groups=mesh['grp'=16,'mem'=8] {'grp','mem'}, dimensions={0} | all-to-all | bytes 3670016 | tf_op jit(solution)/shard_map/all_to_all | solution.py:317
  41.7 0.9 %collective-permute-start = (bf16[1024,896]{1,0:T(8,128)(2,1)S(1)}, bf16[1024,896]{1,0:T(8,128)(2,1)S(1)}, u32[]{:S(2)}, u32[]{:S(2)}) collective-permute-start(bf16[1024,896]{1,0:T(8,128)(2,1)S(1)} %bitcast.9), channel_id=1, source_target_pairs={{0,1},{1,0},{2,3},{3,2},{4,5},{5,4},{6,7},{7,6},{8,9},{9,8},{10,11... | collective-permute-start | bytes 5505032 | tf_op jit(solution)/shard_map/ppermute | solution.py:324
  42.5 3.2 %shard_map.38 = (f32[1,1152]{1,0:T(1,128)S(1)}, f32[8,1152]{1,0:T(8,128)S(1)}) custom-call(bf16[1024,896]{1,0:T(8,128)(2,1)S(1)} %bitcast.10), custom_call_target="tpu_custom_call" | custom-call | tf_op jit(solution)/shard_map/pallas_call | solution.py:187
  45.8 0.0 copy-start.1
  45.8 0.1 collective-permute-done.other_ref
  46.0 1.6 %shard_map.39 = f32[128,128]{1,0:T(8,128)S(1)} custom-call(f32[1,1152]{1,0:T(1,128)S(1)} %get-tuple-element.7.best_ref, f32[8,1152]{1,0:T(8,128)S(1)} %get-tuple-element.8.labels_ref, bf16[1024,896]{1,0:T(8,128)(2,1)S(1)} %bitcast.11, bf16[1024,896]{1,0:T(8,128)(2,1)S(1)} %collective-permute-done.other_ref), custom_call_target="tpu_custom_call" | custom-call | tf_op jit(solution)/shard_map/pallas_call | solution.py:267
  47.6 13.0 %all_to_all.11 = f32[128,1,128]{2,1,0:T(1,128)S(1)} all-to-all(f32[128,1,128]{2,1,0:T(1,128)S(1)} %bitcast.13), channel_id=1, replica_groups=mesh['grp'=16,'mem'=8] {'grp','mem'}, dimensions={0} | all-to-all | bytes 131072 | tf_op jit(solution)/shard_map/all_to_all | solution.py:327
  60.6 0.0 copy-done.1
  60.6 1.1 %shard_map.40 = f32[1,512]{1,0:T(1,128)} custom-call(f32[128,128]{1,0:T(8,128)S(1)} %bitcast.14, s32[1,512]{1,0:T(1,128)S(1)} %bitcast.16), custom_call_target="tpu_custom_call" | custom-call | tf_op jit(solution)/shard_map/pallas_call | solution.py:304
Async XLA Ops:
  0.0 1.2 %copy-start = (bf16[512,768]{1,0:T(8,128)(2,1)S(1)}, bf16[512,768]{1,0:T(8,128)(2,1)}, u32[]{:S(2)}) copy-start(bf16[512,768]{1,0:T(8,128)(2,1)} %embeds_ref.1) | copy-start | bytes 2359300
  41.7 4.3 %collective-permute-start = (bf16[1024,896]{1,0:T(8,128)(2,1)S(1)}, bf16[1024,896]{1,0:T(8,128)(2,1)S(1)}, u32[]{:S(2)}, u32[]{:S(2)}) collective-permute-start(bf16[1024,896]{1,0:T(8,128)(2,1)S(1)} %bitcast.9), channel_id=1, source_target_pairs={{0,1},{1,0},{2,3},{3,2},{4,5},{5,4},{6,7},{7,6},{8,9},{9,8},{10,11... | collective-permute-start | bytes 5505032 | tf_op jit(solution)/shard_map/ppermute | solution.py:324
  45.8 14.8 %copy-start.1 = (s32[512]{0:T(512)S(1)}, s32[512]{0:T(512)}, u32[]{:S(2)}) copy-start(s32[512]{0:T(512)} %param.5) | copy-start | bytes 6148

commit v6 on v5

--- a/solution.py
+++ b/solution.py
@@ -13,7 +13,6 @@
 SPLIT = KEPT // 2
 LANES = 128
 VMEM_LIMIT = 48 * 1024 * 1024
-HIGHEST = lax.Precision.HIGHEST
 
 
 def place(dest, members):
@@ -29,7 +28,7 @@
     core = jnp.where(
         spread, shared // CAP, jnp.where(halved, index // SPLIT, third)
     )
-    chip = jnp.where(spread, 0, 1 + member // 3)
+    chip = jnp.where(spread, members // 2 - 1, (1 + member // 3) % 3)
     row = jnp.where(
         spread, shared % CAP, jnp.where(halved, index % SPLIT, index + SPLIT)
     )
@@ -203,14 +202,15 @@
     slots, wide = rows_ref.shape
     width = wide - LANES
     sources = slots // CAP
-    last_ref[...] = other_ref[:, width:].astype(jnp.float32)
-    labels = last_ref[pl.ds(width // LANES, sources, stride=CAP), :].astype(jnp.bfloat16)
-    column_ref[...] = dot(
-        spread_labels(labels, slots), jnp.ones((LANES, LANES), jnp.bfloat16)
-    )
     block = 256
 
     def run(last_key, first_query):
+        if last_key:
+            last_ref[...] = other_ref[:, width:].astype(jnp.float32)
+            labels = last_ref[pl.ds(width // LANES, sources, stride=CAP), :].astype(jnp.bfloat16)
+            column_ref[...] = dot(
+                spread_labels(labels, slots), jnp.ones((LANES, LANES), jnp.bfloat16)
+            )
         own = [best_ref[:, q : q + block] for q in range(0, slots, block)]
         gained = [jnp.full((1, LANES), -1.0, jnp.float32)] * (slots // LANES)
         for k in range(0, last_key, block):
@@ -251,13 +251,18 @@
             jnp.where(window == (mine + windows // 2) % windows, gained, ninth),
         )
 
-    core = lax.axis_index("mem") % 2
-
-    @pl.when(core == 0)
+    member = lax.axis_index("mem")
+    chip, core = member // 2, member % 2
+
+    @pl.when(chip == 0)
+    def _():
+        run(0, 0)
+
+    @pl.when((chip > 0) & (core == 0))
     def _():
         run(slots // 2, 0)
 
-    @pl.when(core == 1)
+    @pl.when((chip > 0) & (core == 1))
     def _():
         run(slots, slots // 2)
 
@@ -288,11 +293,13 @@
     window = iota((devices, LANES), 1) // CAP
     table = jnp.where(window == mine, jnp.maximum(table, other), table)
     device, row = place(dest_ref[...], members)
-    pick = jnp.where(iota((devices, rows), 0) == device, 1.0, 0.0)
-    found = lax.dot_general(
-        table, pick, (((0,), (0,)), ((), ())), precision=HIGHEST,
-        preferred_element_type=jnp.float32,
-    )
+    pick = ones_where(iota((devices, rows), 0) == device)
+    parts = []
+    left = table.T
+    for _ in range(3):
+        parts.append(left.astype(jnp.bfloat16))
+        left = left - parts[-1].astype(jnp.float32)
+    found = dot(jnp.concatenate(parts, axis=1), jnp.concatenate([pick] * 3, axis=0))
     lane = jnp.where(row < CAP, CAP * mine + row, ninth_lane(me))
     out_ref[...] = jnp.max(
         jnp.where(iota((LANES, rows), 0) == lane, found, -1.0), axis=0, keepdims=True

time: 61.9 us -> 61.6 us (level)
  Pallas kernels: 7.38 us -> 5.68 us
  blocking collectives: 52.1 us -> 53.5 us
    pallas_call x1, Pallas kernels: 1.64 us -> 0.08 us  [cross_best(): pl.pallas_call(cross_kernel, out_shape=jax.ShapeDtypeStruct((slots // CAP...]
    all_to_all x1, blocking collectives: 13 us -> 14.4 us  [shards(): lax.all_to_all(table.reshape(devices, 1, LANES), ('grp', 'mem'), split_ax...]
where the time goes in v6:
time: 61.6 us; the launch traced here: 61.4 us
  blocking collectives  53.5 us (87%)
  Pallas kernels  5.68 us (9%)
  other arithmetic  1.14 us (2%)
  starting transfers between devices  0.87 us (1%)
    all_to_all x1, blocking collectives, shards(): lax.all_to_all(outgoing.reshape(devices, CAP, width + LANES), ('grp', 'me...  39.1 us
    all_to_all x1, blocking collectives, shards(): lax.all_to_all(table.reshape(devices, 1, LANES), ('grp', 'mem'), split_ax...  14.4 us
    pallas_call x1, Pallas kernels, own_best(): pl.pallas_call(own_kernel, out_shape=(jax.ShapeDtypeStruct((1, count), jn...  3.25 us
    pallas_call x1, Pallas kernels, pack(): pl.pallas_call(pack_kernel, out_shape=jax.ShapeDtypeStruct((slots, width...  1.41 us
  transfers between devices with their start and end apart: 1, of which 1 were waited for; matrix products, arithmetic and copies ran while one was open for 0% of the time, Pallas kernels for 5%

profile of v6, /device:TPU:1, one launch (start us, length us, event | category | flops | bytes accessed | tf_op | source)
XLA Modules:
  0.0 61.4 jit_solution(14188413945867427188)
XLA Ops:
  0.0 0.0 copy-start
  0.0 0.8 %multiply_add_fusion = (s32[512]{0:T(512)S(1)}, s32[512]{0:T(512)S(1)}) fusion(s32[512]{0:T(512)} %param.4, s32[512]{0:T(512)} %param.5), kind=kLoop, calls=%fused_computation.31 | loop fusion | flops 56832 | bytes 8192 | tf_op jit(solution)/shard_map/add | solution.py:96
  0.8 0.3 fusion.pick_ref
  1.2 0.0 copy-done
  1.2 1.4 %shard_map.37 = bf16[1024,896]{1,0:T(8,128)(2,1)S(1)} custom-call(bf16[512,768]{1,0:T(8,128)(2,1)S(1)} %copy-done, s32[1,512]{1,0:T(1,128)S(1)} %bitcast.15, f32[1152,512]{1,0:T(8,128)S(1)} %fusion.pick_ref), custom_call_target="tpu_custom_call" | custom-call | tf_op jit(solution)/shard_map/pallas_call | solution.py:98
  2.6 39.1 %all_to_all.10 = bf16[128,8,896]{2,1,0:T(8,128)(2,1)S(1)} all-to-all(bf16[128,8,896]{2,1,0:T(8,128)(2,1)S(1)} %bitcast.12), channel_id=1, replica_groups=mesh['grp'=16,'mem'=8] {'grp','mem'}, dimensions={0} | all-to-all | bytes 3670016 | tf_op jit(solution)/shard_map/all_to_all | solution.py:324
  41.7 0.9 %collective-permute-start = (bf16[1024,896]{1,0:T(8,128)(2,1)S(1)}, bf16[1024,896]{1,0:T(8,128)(2,1)S(1)}, u32[]{:S(2)}, u32[]{:S(2)}) collective-permute-start(bf16[1024,896]{1,0:T(8,128)(2,1)S(1)} %bitcast.9), channel_id=1, source_target_pairs={{0,1},{1,0},{2,3},{3,2},{4,5},{5,4},{6,7},{7,6},{8,9},{9,8},{10,11... | collective-permute-start | bytes 5505032 | tf_op jit(solution)/shard_map/ppermute | solution.py:331
  42.5 3.2 %shard_map.38 = (f32[1,1152]{1,0:T(1,128)S(1)}, f32[8,1152]{1,0:T(8,128)S(1)}) custom-call(bf16[1024,896]{1,0:T(8,128)(2,1)S(1)} %bitcast.10), custom_call_target="tpu_custom_call" | custom-call | tf_op jit(solution)/shard_map/pallas_call | solution.py:186
  45.8 0.0 copy-start.1
  45.8 0.1 collective-permute-done.other_ref
  46.0 0.1 shard_map.39
  46.0 14.4 %all_to_all.11 = f32[128,1,128]{2,1,0:T(1,128)S(1)} all-to-all(f32[128,1,128]{2,1,0:T(1,128)S(1)} %bitcast.13), channel_id=1, replica_groups=mesh['grp'=16,'mem'=8] {'grp','mem'}, dimensions={0} | all-to-all | bytes 131072 | tf_op jit(solution)/shard_map/all_to_all | solution.py:334
  60.5 0.0 copy-done.1
  60.5 0.9 %shard_map.40 = f32[1,512]{1,0:T(1,128)} custom-call(f32[128,128]{1,0:T(8,128)S(1)} %bitcast.14, s32[1,512]{1,0:T(1,128)S(1)} %bitcast.16), custom_call_target="tpu_custom_call" | custom-call | tf_op jit(solution)/shard_map/pallas_call | solution.py:311
Async XLA Ops:
  0.0 1.2 %copy-start = (bf16[512,768]{1,0:T(8,128)(2,1)S(1)}, bf16[512,768]{1,0:T(8,128)(2,1)}, u32[]{:S(2)}) copy-start(bf16[512,768]{1,0:T(8,128)(2,1)} %embeds_ref.1) | copy-start | bytes 2359300
  41.7 4.3 %collective-permute-start = (bf16[1024,896]{1,0:T(8,128)(2,1)S(1)}, bf16[1024,896]{1,0:T(8,128)(2,1)S(1)}, u32[]{:S(2)}, u32[]{:S(2)}) collective-permute-start(bf16[1024,896]{1,0:T(8,128)(2,1)S(1)} %bitcast.9), channel_id=1, source_target_pairs={{0,1},{1,0},{2,3},{3,2},{4,5},{5,4},{6,7},{7,6},{8,9},{9,8},{10,11... | collective-permute-start | bytes 5505032 | tf_op jit(solution)/shard_map/ppermute | solution.py:331
  45.8 14.7 %copy-start.1 = (s32[512]{0:T(512)S(1)}, s32[512]{0:T(512)}, u32[]{:S(2)}) copy-start(s32[512]{0:T(512)} %param.5) | copy-start | bytes 6148

commit v7 on v6

v7 whole, which is shorter than its diff:
```python
import functools

import jax
import jax.numpy as jnp
from jax import lax
from jax.experimental import pallas as pl
from jax.experimental.pallas import tpu as pltpu
from jax.sharding import PartitionSpec as P

CAP = 8
SHARED = 2
KEPT = CAP - SHARED
SPLIT = KEPT // 2
LANES = 128
VMEM_LIMIT = 48 * 1024 * 1024


def place(dest, members):
    owner = dest // CAP
    group = owner // members
    member = owner % members
    column = dest % CAP
    shared = member * SHARED + column
    index = column - SHARED
    third = member % 3
    halved = third == 2
    spread = column < SHARED
    core = jnp.where(
        spread, shared // CAP, jnp.where(halved, index // SPLIT, third)
    )
    chip = jnp.where(spread, 0, 1 + member // 3)
    row = jnp.where(
        spread, shared % CAP, jnp.where(halved, index % SPLIT, index + SPLIT)
    )
    return group, 2 * chip + core, row


def swap_cores(members):
    return [(member, member ^ 1) for member in range(members)]


def params():
    return pltpu.CompilerParams(vmem_limit_bytes=VMEM_LIMIT)


def iota(shape, axis):
    return lax.broadcasted_iota(jnp.int32, shape, axis)


def dot(a, b):
    return jnp.dot(a, b, preferred_element_type=jnp.float32)


def dot_t(a, b):
    return lax.dot_general(a, b, (((1,), (1,)), ((), ())), preferred_element_type=jnp.float32)


def ones_where(mask):
    return jnp.where(mask, 1.0, 0.0).astype(jnp.bfloat16)


def pack_kernel(embeds_ref, packed_ref, pick_ref, out_ref, unit_ref, last_ref):
    rows, width = embeds_ref.shape
    slots = out_ref.shape[0]
    devices = slots // CAP
    packed = packed_ref[...]
    spot = packed % (2 * slots)
    label = (packed // (2 * slots)).astype(jnp.float32)
    device = jnp.where(spot < slots, spot // CAP, spot - slots)
    row = jnp.where(spot < slots, spot % CAP, CAP)

    values = embeds_ref[...].astype(jnp.float32)
    total = jnp.sum(values * values, axis=1, keepdims=True)
    unit_ref[...] = (values * lax.rsqrt(total + 1e-06)).astype(jnp.bfloat16)

    ninth = dot(pick_ref[slots:, :].astype(jnp.bfloat16), unit_ref[...])
    for piece in range(width // LANES):
        last_ref[pl.ds(piece, devices, stride=CAP), :] = ninth[
            :, piece * LANES : (piece + 1) * LANES
        ]
    here = ones_where(iota((devices, rows), 0) == device)
    marks = jnp.where(iota((LANES, rows), 0) == row, label, 0.0).astype(jnp.bfloat16)
    labels = dot_t(here, marks)
    for piece in range(width // LANES, CAP):
        last_ref[pl.ds(piece, devices, stride=CAP), :] = labels
    out_ref[:, width:] = last_ref[...].astype(jnp.bfloat16)

    block = 256
    for b in range(0, slots, block):
        out_ref[b : b + block, :width] = dot(pick_ref[b : b + block, :].astype(jnp.bfloat16), unit_ref[...]).astype(
            jnp.bfloat16
        )


def pack(embeds, cluster, dest, slots, members):
    rows, width = embeds.shape
    devices = slots // CAP
    group, member, row = place(dest, members)
    device = member * (devices // members) + group
    spot = jnp.where(row < CAP, device * CAP + row, slots + device)
    packed = (spot + 2 * slots * (cluster + 1)).reshape(1, rows)
    pick = jnp.where(iota((slots + devices, rows), 0) == spot[None], 1.0, 0.0)
    return pl.pallas_call(
        pack_kernel,
        out_shape=jax.ShapeDtypeStruct((slots, width + LANES), jnp.bfloat16),
        scratch_shapes=[
            pltpu.VMEM((rows, width), jnp.bfloat16),
            pltpu.VMEM((slots, LANES), jnp.float32),
        ],
        compiler_params=params(),
    )(embeds, packed, pick)


def ninth_lane(group, member):
    return CAP * ((group + 1) % (LANES // CAP)) + member


def spread_labels(labels, slots):
    row = iota((slots, LANES), 0)
    lane = iota((slots, LANES), 1)
    repeat = ones_where(iota((slots, len(labels)), 0) // CAP == iota((slots, len(labels)), 1))
    return jnp.where(lane == row % CAP, dot(repeat, labels), 0.0).astype(
        jnp.bfloat16
    )


def widen(widest, scores):
    for lane in range(0, scores.shape[1], LANES):
        widest = jnp.maximum(widest, scores[:, lane : lane + LANES])
    return widest


def across(widest):
    return jnp.concatenate(
        [
            jnp.max(widest[j : j + LANES].T, axis=0, keepdims=True)
            for j in range(0, widest.shape[0], LANES)
        ],
        axis=1,
    )


def own_kernel(rows_ref, best_ref, labels_ref, last_ref, ninth_ref, column_ref):
    slots, wide = rows_ref.shape
    width = wide - LANES
    sources = slots // CAP
    last_ref[...] = rows_ref[:, width:].astype(jnp.float32)
    for piece in range(width // LANES):
        ninth_ref[:, piece * LANES : (piece + 1) * LANES] = last_ref[
            pl.ds(piece, sources, stride=CAP), :
        ].astype(jnp.bfloat16)
    labels = last_ref[pl.ds(width // LANES, sources, stride=CAP), :].astype(jnp.bfloat16)
    spots = spread_labels(labels, slots)
    groups = LANES // CAP
    source = iota((sources, LANES), 1)
    order = ones_where(
        iota((sources, LANES), 0) == ninth_lane(source % groups, source // groups)
    )
    ninth_ref[...] = dot(order, ninth_ref[...]).astype(jnp.bfloat16)
    labels = dot(order, labels).astype(jnp.bfloat16)
    ones = jnp.ones((LANES, LANES), jnp.bfloat16)
    column_ref[:slots, :] = dot(spots, ones)
    at_ninth = ones_where(iota((LANES, LANES), 0) == CAP)
    column_ref[slots:, :] = dot(labels, at_ninth)
    at_ninth = ones_where(iota((CAP, LANES), 1) == CAP)
    row_labels = jnp.concatenate(
        [dot_t(ones[:CAP], spots), dot_t(at_ninth, labels)], axis=1
    )
    labels_ref[...] = row_labels

    block = 256
    starts = list(range(0, slots, block)) + [slots]
    sizes = [block] * (slots // block) + [sources]

    def read(i):
        if starts[i] == slots:
            return ninth_ref[...]
        return rows_ref[starts[i] : starts[i] + block, :width]

    best = [jnp.full((1, size), -1.0, jnp.float32) for size in sizes]
    for k, (key, count) in enumerate(zip(starts, sizes)):
        widest = jnp.full((count, LANES), -1.0, jnp.float32)
        keys = read(k)
        for q in range(k, len(starts)):
            query, size = starts[q], sizes[q]
            scores = dot_t(keys, read(q))
            same = column_ref[key : key + count, :1] == row_labels[:1, query : query + size]
            if q == k:
                same = same & (iota((count, size), 0) != iota((count, size), 1))
            scores = jnp.where(same, scores, -1.0)
            best[q] = jnp.maximum(best[q], jnp.max(scores, axis=0, keepdims=True))
            if q > k:
                widest = widen(widest, scores)
        if k + 1 < len(starts):
            best[k] = jnp.maximum(best[k], across(widest))
        best_ref[:, key : key + count] = best[k]


def own_best(arrived):
    slots, wide = arrived.shape
    count = slots + slots // CAP
    return pl.pallas_call(
        own_kernel,
        out_shape=(
            jax.ShapeDtypeStruct((1, count), jnp.float32),
            jax.ShapeDtypeStruct((CAP, count), jnp.float32),
        ),
        scratch_shapes=[
            pltpu.VMEM((slots, LANES), jnp.float32),
            pltpu.VMEM((slots // CAP, wide - LANES), jnp.bfloat16),
            pltpu.VMEM((count, LANES), jnp.float32),
        ],
        compiler_params=params(),
    )(arrived)


FIRST = ({0: (0, 2, 3), 1: (0, 2, 3)}, {0: (2, 3), 1: (0, 1, 2, 3)})
SECOND = ({2: (2,), 3: (2,)}, {3: (2, 3)})
BLOCKS = 4


def on_each_core(run, plans):
    member = lax.axis_index("mem")
    core = member % 2
    alone = member // 2 == lax.axis_size("mem") // 2 - 1
    pl.when(alone)(lambda: run({}))
    for index, plan in enumerate(plans):
        pl.when(jnp.logical_not(alone) & (core == index))(functools.partial(run, plan))


def meet(plan, best_ref, labels_ref, rows_ref, other_ref, last_ref, column_ref):
    slots, wide = rows_ref.shape
    width = wide - LANES
    block = slots // BLOCKS
    half = other_ref.shape[0]
    if plan:
        last_ref[...] = other_ref[:, width:].astype(jnp.float32)
        labels = last_ref[pl.ds(width // LANES, half // CAP, stride=CAP), :].astype(jnp.bfloat16)
        column_ref[...] = dot(
            spread_labels(labels, half), jnp.ones((LANES, LANES), jnp.bfloat16)
        )
    own = [best_ref[:, q * block : (q + 1) * block] for q in range(BLOCKS)]
    gained = [jnp.full((1, block), -1.0, jnp.float32)] * (BLOCKS // 2)
    for k, queries in plan.items():
        first = k * block % half
        keys = other_ref[first : first + block, :width]
        key_labels = column_ref[first : first + block, :1]
        widest = jnp.full((block, LANES), -1.0, jnp.float32)
        for q in queries:
            scores = dot_t(keys, rows_ref[q * block : (q + 1) * block, :width])
            same = key_labels == labels_ref[:1, q * block : (q + 1) * block]
            scores = jnp.where(same, scores, -1.0)
            own[q] = jnp.maximum(own[q], jnp.max(scores, axis=0, keepdims=True))
            widest = widen(widest, scores)
        gained[k % (BLOCKS // 2)] = across(widest)
    return jnp.concatenate(own, axis=1), jnp.concatenate(gained, axis=1)


def first_kernel(
    best_ref, labels_ref, rows_ref, other_ref, out_ref, gained_ref, last_ref, column_ref
):
    slots = rows_ref.shape[0]

    def run(plan):
        own, gained = meet(
            plan, best_ref, labels_ref, rows_ref, other_ref, last_ref, column_ref
        )
        out_ref[:, :slots] = own
        out_ref[:, slots:] = best_ref[:, slots:]
        gained_ref[...] = gained

    on_each_core(run, FIRST)


def second_kernel(
    best_ref, gained_ref, labels_ref, rows_ref, other_ref, out_ref, last_ref, column_ref
):
    slots = rows_ref.shape[0]
    groups = LANES // CAP
    shape = (groups, LANES)

    def run(plan):
        own, gained = meet(
            plan, best_ref, labels_ref, rows_ref, other_ref, last_ref, column_ref
        )
        gained = jnp.concatenate([gained_ref[...], gained], axis=1)
        window = iota(shape, 1) // CAP
        mine = iota(shape, 0)
        ninth = jnp.broadcast_to(best_ref[:, slots:], shape)
        for first in range(0, slots, LANES):
            tile = slice(first, first + LANES)
            turned = pltpu.roll(jnp.broadcast_to(gained[:, tile], shape), LANES // 2, 1)
            out_ref[first // CAP : first // CAP + groups, :] = jnp.where(
                window == mine,
                jnp.broadcast_to(own[:, tile], shape),
                jnp.where(window == (mine + groups // 2) % groups, turned, ninth),
            )

    on_each_core(run, SECOND)


def cross_best(best, labels, arrived, others):
    slots = arrived.shape[0]
    half = slots // 2
    scratch = [pltpu.VMEM((half, LANES), jnp.float32)] * 2
    best, gained = pl.pallas_call(
        first_kernel,
        out_shape=(
            jax.ShapeDtypeStruct(best.shape, jnp.float32),
            jax.ShapeDtypeStruct((1, half), jnp.float32),
        ),
        scratch_shapes=scratch,
        compiler_params=params(),
    )(best, labels, arrived, others[0])
    return pl.pallas_call(
        second_kernel,
        out_shape=jax.ShapeDtypeStruct((slots // CAP, LANES), jnp.float32),
        scratch_shapes=scratch,
        compiler_params=params(),
    )(best, gained, labels, arrived, others[1])


def lookup_kernel(members, table_ref, dest_ref, out_ref):
    devices = table_ref.shape[0]
    rows = dest_ref.shape[1]
    mine = lax.axis_index("grp")
    groups = devices // members
    table = table_ref[...]
    turned = pltpu.roll(table, LANES // 2, 1)
    core = iota((devices, LANES), 0) // groups % 2
    other = jnp.where(
        core == 0, pltpu.roll(turned, devices - groups, 0), pltpu.roll(turned, groups, 0)
    )
    window = iota((devices, LANES), 1) // CAP
    table = jnp.where(window == mine, jnp.maximum(table, other), table)
    group, member, row = place(dest_ref[...], members)
    pick = ones_where(iota((devices, rows), 0) == member * groups + group)
    parts = []
    left = table.T
    for _ in range(3):
        parts.append(left.astype(jnp.bfloat16))
        left = left - parts[-1].astype(jnp.float32)
    found = dot(jnp.concatenate(parts, axis=1), jnp.concatenate([pick] * 3, axis=0))
    lane = jnp.where(row < CAP, CAP * mine + row, ninth_lane(mine, lax.axis_index("mem")))
    out_ref[...] = jnp.max(
        jnp.where(iota((LANES, rows), 0) == lane, found, -1.0), axis=0, keepdims=True
    )


def lookup(table, dest, members):
    rows = dest.shape[0]
    return pl.pallas_call(
        functools.partial(lookup_kernel, members),
        out_shape=jax.ShapeDtypeStruct((1, rows), jnp.float32),
        compiler_params=params(),
    )(table, dest.reshape(1, rows)).reshape(rows)


def shards(embeds, cluster, dest):
    members = lax.axis_size("mem")
    devices = lax.axis_size("grp") * members
    width = embeds.shape[1]
    slots = devices * CAP
    outgoing = pack(embeds, cluster, dest, slots, members)
    arrived = lax.all_to_all(
        outgoing.reshape(devices, CAP, width + LANES),
        ("mem", "grp"),
        split_axis=0,
        concat_axis=0,
        tiled=True,
    ).reshape(slots, width + LANES)
    half = slots // 2
    others = [
        lax.ppermute(arrived[first : first + half], "mem", swap_cores(members))
        for first in (0, half)
    ]
    best, labels = own_best(arrived)
    table = cross_best(best, labels, arrived, others)
    returned = lax.all_to_all(
        table.reshape(devices, 1, LANES),
        ("mem", "grp"),
        split_axis=0,
        concat_axis=0,
        tiled=True,
    ).reshape(devices, LANES)
    return lookup(returned, dest, members)


def solution(mesh):
    placed = (P(("grp", "mem"), None), P(("grp", "mem")), P(("grp", "mem")))
    return jax.shard_map(
        shards, mesh=mesh, in_specs=placed, out_specs=P(("grp", "mem")), check_vma=False
    )
```

time: 61.6 us -> 60.4 us (0.981)
  blocking collectives: 53.5 us -> 51 us
  starting transfers between devices: 0.87 us -> 1.55 us
  Pallas kernels: 5.68 us -> 6.3 us
    all_to_all x2, blocking collectives: 53.5 us -> 51 us  [the longest x1 38.1 us: shards(): lax.all_to_all(outgoing.reshape(devices, CAP, width + LANES), ('mem', 'gr...]
    pallas_call x1 -> x2, Pallas kernels: 0.08 us -> 1.75 us  [the longest x1 1.05 us: cross_best(): pl.pallas_call(first_kernel, out_shape=(jax.ShapeDtypeStruct(best.shape,...]
    pallas_call x1, Pallas kernels: 3.25 us -> 2.2 us  [own_best(): pl.pallas_call(own_kernel, out_shape=(jax.ShapeDtypeStruct((1, count), jn...]
    ppermute x1 -> x2, starting transfers between devices: 0.87 us -> 1.55 us  [shards(): lax.ppermute(arrived[first:first + half], 'mem', swap_cores(members))]
  transfers between devices with their start and end apart: 1 -> 2, of which waited for: 1 -> 0; matrix products, arithmetic and copies ran while one was open for 0% -> 0% of each run, Pallas kernels for 5% -> 5%
where the time goes in v7:
time: 60.4 us; the launch traced here: 60.3 us
  blocking collectives  51 us (84%)
  Pallas kernels  6.3 us (10%)
  starting transfers between devices  1.55 us (3%)
  other arithmetic  1.13 us (2%)
    all_to_all x1, blocking collectives, shards(): lax.all_to_all(outgoing.reshape(devices, CAP, width + LANES), ('mem', 'gr...  38.1 us
    all_to_all x1, blocking collectives, shards(): lax.all_to_all(table.reshape(devices, 1, LANES), ('mem', 'grp'), split_ax...  12.9 us
    pallas_call x1, Pallas kernels, own_best(): pl.pallas_call(own_kernel, out_shape=(jax.ShapeDtypeStruct((1, count), jn...  2.2 us
    ppermute x2, starting transfers between devices, shards(): lax.ppermute(arrived[first:first + half], 'mem', swap_cores(members))  1.55 us
    pallas_call x1, Pallas kernels, pack(): pl.pallas_call(pack_kernel, out_shape=jax.ShapeDtypeStruct((slots, width...  1.41 us
  transfers between devices with their start and end apart: 2, of which 0 were waited for; matrix products, arithmetic and copies ran while one was open for 0% of the time, Pallas kernels for 5%

profile of v7, /device:TPU:1, one launch (start us, length us, event | category | flops | bytes accessed | tf_op | source)
XLA Modules:
  0.0 60.3 jit_solution(9934401931484401460)
XLA Ops:
  0.0 0.0 copy-start
  0.0 0.8 %multiply_add_fusion = (s32[512]{0:T(512)S(1)}, s32[512]{0:T(512)S(1)}) fusion(s32[512]{0:T(512)} %param.4, s32[512]{0:T(512)} %param.5), kind=kLoop, calls=%fused_computation.28 | loop fusion | flops 53760 | bytes 8192 | tf_op jit(solution)/shard_map/add | solution.py:101
  0.8 0.3 fusion.pick_ref
  1.1 0.0 copy-done
  1.2 1.4 %shard_map.37 = bf16[1024,896]{1,0:T(8,128)(2,1)S(1)} custom-call(bf16[512,768]{1,0:T(8,128)(2,1)S(1)} %copy-done, s32[1,512]{1,0:T(1,128)S(1)} %bitcast.19, f32[1152,512]{1,0:T(8,128)S(1)} %fusion.pick_ref), custom_call_target="tpu_custom_call" | custom-call | tf_op jit(solution)/shard_map/pallas_call | solution.py:103
  2.6 38.1 %all_to_all.10 = bf16[128,8,896]{2,1,0:T(8,128)(2,1)S(1)} all-to-all(bf16[128,8,896]{2,1,0:T(8,128)(2,1)S(1)} %bitcast.16), channel_id=1, replica_groups=mesh['grp'=16,'mem'=8] {'mem','grp'}, dimensions={0} | all-to-all | bytes 3670016 | tf_op jit(solution)/shard_map/all_to_all | solution.py:365
  40.7 0.1 slice_bitcast_fusion
  40.8 1.5 %collective-permute-start = (bf16[512,896]{1,0:T(8,128)(2,1)S(1)}, bf16[512,896]{1,0:T(8,128)(2,1)S(1)}, u32[]{:S(2)}, u32[]{:S(2)}) collective-permute-start(bf16[512,896]{1,0:T(8,128)(2,1)S(1)} %get-tuple-element.16), channel_id=1, source_target_pairs={{0,1},{1,0},{2,3},{3,2},{4,5},{5,4},{6,7},{7,6},{8,9},{9,8},{10,11... | collective-permute-start | bytes 2752520 | tf_op jit(solution)/shard_map/ppermute | solution.py:374
  42.3 0.1 collective-permute-start.1
  42.4 2.2 %shard_map.38 = (f32[1,1152]{1,0:T(1,128)S(1)}, f32[8,1152]{1,0:T(8,128)S(1)}) custom-call(bf16[1024,896]{1,0:T(8,128)(2,1)S(1)} %bitcast.13), custom_call_target="tpu_custom_call" | custom-call | tf_op jit(solution)/shard_map/pallas_call | solution.py:202
  44.6 0.0 collective-permute-done.other_ref
  44.6 0.0 copy-start.1
  44.6 1.1 %shard_map.39 = (f32[1,1152]{1,0:T(1,128)S(1)}, f32[1,512]{1,0:T(1,128)S(1)}) custom-call(f32[1,1152]{1,0:T(1,128)S(1)} %get-tuple-element.9.best_ref, f32[8,1152]{1,0:T(8,128)S(1)} %get-tuple-element.10.labels_ref, bf16[1024,896]{1,0:T(8,128)(2,1)S(1)} %bitcast.14, bf16[512,896]{1,0:T(8,128)(2,1)S(1)} %collective-permute-done.other_ref), custom_call_target="tpu_custom_call" | custom-call | tf_op jit(solution)/shard_map/pallas_call | solution.py:306
  45.7 0.0 collective-permute-done.1.other_ref
  45.7 0.7 %shard_map.40 = f32[128,128]{1,0:T(8,128)S(1)} custom-call(f32[1,1152]{1,0:T(1,128)S(1)} %get-tuple-element.11.best_ref, f32[1,512]{1,0:T(1,128)S(1)} %get-tuple-element.12.gained_ref, f32[8,1152]{1,0:T(8,128)S(1)} %get-tuple-element.10.labels_ref, bf16[1024,896]{1,0:T(8,128)(2,1)S(1)} %bitcast.15, bf16[512,896]{1,0:T(8,128)(2,1)S(1)} %collective-permute-done.1.other_ref), custom_call_target="tpu_custom_call" | custom-call | tf_op jit(solution)/shard_map/pallas_call | solution.py:315
  46.4 12.9 %all_to_all.11 = f32[128,1,128]{2,1,0:T(1,128)S(1)} all-to-all(f32[128,1,128]{2,1,0:T(1,128)S(1)} %bitcast.17), channel_id=1, replica_groups=mesh['grp'=16,'mem'=8] {'mem','grp'}, dimensions={0} | all-to-all | bytes 131072 | tf_op jit(solution)/shard_map/all_to_all | solution.py:379
  59.3 0.0 copy-done.1
  59.3 0.9 %shard_map.41 = f32[1,512]{1,0:T(1,128)} custom-call(f32[128,128]{1,0:T(8,128)S(1)} %bitcast.18, s32[1,512]{1,0:T(1,128)S(1)} %bitcast.20), custom_call_target="tpu_custom_call" | custom-call | tf_op jit(solution)/shard_map/pallas_call | solution.py:352
Async XLA Ops:
  0.0 1.2 %copy-start = (bf16[512,768]{1,0:T(8,128)(2,1)S(1)}, bf16[512,768]{1,0:T(8,128)(2,1)}, u32[]{:S(2)}) copy-start(bf16[512,768]{1,0:T(8,128)(2,1)} %embeds_ref.1) | copy-start | bytes 2359300
  40.8 3.8 %collective-permute-start = (bf16[512,896]{1,0:T(8,128)(2,1)S(1)}, bf16[512,896]{1,0:T(8,128)(2,1)S(1)}, u32[]{:S(2)}, u32[]{:S(2)}) collective-permute-start(bf16[512,896]{1,0:T(8,128)(2,1)S(1)} %get-tuple-element.16), channel_id=1, source_target_pairs={{0,1},{1,0},{2,3},{3,2},{4,5},{5,4},{6,7},{7,6},{8,9},{9,8},{10,11... | collective-permute-start | bytes 2752520 | tf_op jit(solution)/shard_map/ppermute | solution.py:374
  42.3 3.4 %collective-permute-start.1 = (bf16[512,896]{1,0:T(8,128)(2,1)S(1)}, bf16[512,896]{1,0:T(8,128)(2,1)S(1)}, u32[]{:S(2)}, u32[]{:S(2)}) collective-permute-start(bf16[512,896]{1,0:T(8,128)(2,1)S(1)} %get-tuple-element.15), channel_id=1, source_target_pairs={{0,1},{1,0},{2,3},{3,2},{4,5},{5,4},{6,7},{7,6},{8,9},{9,8},{10,11... | collective-permute-start | bytes 2752520 | tf_op jit(solution)/shard_map/ppermute | solution.py:374
  44.6 14.7 %copy-start.1 = (s32[512]{0:T(512)S(1)}, s32[512]{0:T(512)}, u32[]{:S(2)}) copy-start(s32[512]{0:T(512)} %param.5) | copy-start | bytes 6148

commit v8 on v7

--- a/solution.py
+++ b/solution.py
@@ -59,56 +59,72 @@
     return jnp.where(mask, 1.0, 0.0).astype(jnp.bfloat16)
 
 
-def pack_kernel(embeds_ref, packed_ref, pick_ref, out_ref, unit_ref, last_ref):
+def pack_kernel(
+    members, embeds_hbm, cluster_hbm, dest_hbm, out_ref,
+    embeds_ref, cluster_ref, dest_ref, unit_ref, last_ref, sems,
+):
     rows, width = embeds_ref.shape
     slots = out_ref.shape[0]
     devices = slots // CAP
-    packed = packed_ref[...]
-    spot = packed % (2 * slots)
-    label = (packed // (2 * slots)).astype(jnp.float32)
-    device = jnp.where(spot < slots, spot // CAP, spot - slots)
-    row = jnp.where(spot < slots, spot % CAP, CAP)
-
+    block = 256
+    copies = [
+        pltpu.make_async_copy(source, target, sems.at[index])
+        for index, (source, target) in enumerate(
+            ((dest_hbm, dest_ref), (cluster_hbm, cluster_ref), (embeds_hbm, embeds_ref))
+        )
+    ]
+    for copy in copies:
+        copy.start()
+    copies[0].wait()
+    copies[1].wait()
+    group, member, row = place(dest_ref[...], members)
+    device = member * (devices // members) + group
+    slot = jnp.where(row < CAP, device * CAP + row, -1)
+    picks = [ones_where(b + iota((block, rows), 0) == slot) for b in range(0, slots, block)]
+    here = iota((devices, rows), 0) == device
+    pick_ninth = ones_where(here & (row == CAP))
+    label = (cluster_ref[...] + 1).astype(jnp.float32)
+    marks = jnp.where(iota((LANES, rows), 0) == row, label, 0.0).astype(jnp.bfloat16)
+    labels = dot_t(ones_where(here), marks)
+    for piece in range(width // LANES, CAP):
+        last_ref[pl.ds(piece, devices, stride=CAP), :] = labels
+
+    copies[2].wait()
     values = embeds_ref[...].astype(jnp.float32)
     total = jnp.sum(values * values, axis=1, keepdims=True)
     unit_ref[...] = (values * lax.rsqrt(total + 1e-06)).astype(jnp.bfloat16)
-
-    ninth = dot(pick_ref[slots:, :].astype(jnp.bfloat16), unit_ref[...])
+    for b, pick in enumerate(picks):
+        out_ref[b * block : (b + 1) * block, :width] = dot(pick, unit_ref[...]).astype(
+            jnp.bfloat16
+        )
+    ninth = dot(pick_ninth, unit_ref[...])
     for piece in range(width // LANES):
         last_ref[pl.ds(piece, devices, stride=CAP), :] = ninth[
             :, piece * LANES : (piece + 1) * LANES
         ]
-    here = ones_where(iota((devices, rows), 0) == device)
-    marks = jnp.where(iota((LANES, rows), 0) == row, label, 0.0).astype(jnp.bfloat16)
-    labels = dot_t(here, marks)
-    for piece in range(width // LANES, CAP):
-        last_ref[pl.ds(piece, devices, stride=CAP), :] = labels
     out_ref[:, width:] = last_ref[...].astype(jnp.bfloat16)
-
-    block = 256
-    for b in range(0, slots, block):
-        out_ref[b : b + block, :width] = dot(pick_ref[b : b + block, :].astype(jnp.bfloat16), unit_ref[...]).astype(
-            jnp.bfloat16
-        )
 
 
 def pack(embeds, cluster, dest, slots, members):
     rows, width = embeds.shape
-    devices = slots // CAP
-    group, member, row = place(dest, members)
-    device = member * (devices // members) + group
-    spot = jnp.where(row < CAP, device * CAP + row, slots + device)
-    packed = (spot + 2 * slots * (cluster + 1)).reshape(1, rows)
-    pick = jnp.where(iota((slots + devices, rows), 0) == spot[None], 1.0, 0.0)
+    operands = [
+        pltpu.with_memory_space_constraint(operand, pltpu.HBM)
+        for operand in (embeds, cluster.reshape(1, rows), dest.reshape(1, rows))
+    ]
     return pl.pallas_call(
-        pack_kernel,
+        functools.partial(pack_kernel, members),
         out_shape=jax.ShapeDtypeStruct((slots, width + LANES), jnp.bfloat16),
+        in_specs=[pl.BlockSpec(memory_space=pltpu.HBM)] * 3,
         scratch_shapes=[
             pltpu.VMEM((rows, width), jnp.bfloat16),
+            pltpu.VMEM((1, rows), jnp.int32),
+            pltpu.VMEM((1, rows), jnp.int32),
+            pltpu.VMEM((rows, width), jnp.bfloat16),
             pltpu.VMEM((slots, LANES), jnp.float32),
+            pltpu.SemaphoreType.DMA((3,)),
         ],
         compiler_params=params(),
-    )(embeds, packed, pick)
+    )(*operands)
 
 
 def ninth_lane(group, member):
@@ -122,6 +138,23 @@
     return jnp.where(lane == row % CAP, dot(repeat, labels), 0.0).astype(
         jnp.bfloat16
     )
+
+
+def in_every_lane(spots):
+    return jnp.broadcast_to(
+        jnp.sum(spots.astype(jnp.float32), axis=1, keepdims=True), spots.shape
+    )
+
+
+def masked(scores, key_labels, query_labels, skip=False):
+    count, size = scores.shape
+    tiles = []
+    for lane in range(0, size, LANES):
+        same = key_labels == query_labels[:, lane : lane + LANES]
+        if skip:
+            same = same & (iota((count, LANES), 0) != iota((count, LANES), 1) + lane)
+        tiles.append(jnp.where(same, scores[:, lane : lane + LANES], -1.0))
+    return jnp.concatenate(tiles, axis=1)
 
 
 def widen(widest, scores):
@@ -159,7 +192,7 @@
     ninth_ref[...] = dot(order, ninth_ref[...]).astype(jnp.bfloat16)
     labels = dot(order, labels).astype(jnp.bfloat16)
     ones = jnp.ones((LANES, LANES), jnp.bfloat16)
-    column_ref[:slots, :] = dot(spots, ones)
+    column_ref[:slots, :] = in_every_lane(spots)
     at_ninth = ones_where(iota((LANES, LANES), 0) == CAP)
     column_ref[slots:, :] = dot(labels, at_ninth)
     at_ninth = ones_where(iota((CAP, LANES), 1) == CAP)
@@ -183,11 +216,12 @@
         keys = read(k)
         for q in range(k, len(starts)):
             query, size = starts[q], sizes[q]
-            scores = dot_t(keys, read(q))
-            same = column_ref[key : key + count, :1] == row_labels[:1, query : query + size]
-            if q == k:
-                same = same & (iota((count, size), 0) != iota((count, size), 1))
-            scores = jnp.where(same, scores, -1.0)
+            scores = masked(
+                dot_t(keys, read(q)),
+                column_ref[key : key + count, :],
+                row_labels[:1, query : query + size],
+                q == k,
+            )
             best[q] = jnp.maximum(best[q], jnp.max(scores, axis=0, keepdims=True))
             if q > k:
                 widest = widen(widest, scores)
@@ -236,20 +270,20 @@
     if plan:
         last_ref[...] = other_ref[:, width:].astype(jnp.float32)
         labels = last_ref[pl.ds(width // LANES, half // CAP, stride=CAP), :].astype(jnp.bfloat16)
-        column_ref[...] = dot(
-            spread_labels(labels, half), jnp.ones((LANES, LANES), jnp.bfloat16)
-        )
+        column_ref[...] = in_every_lane(spread_labels(labels, half))
     own = [best_ref[:, q * block : (q + 1) * block] for q in range(BLOCKS)]
     gained = [jnp.full((1, block), -1.0, jnp.float32)] * (BLOCKS // 2)
     for k, queries in plan.items():
         first = k * block % half
         keys = other_ref[first : first + block, :width]
-        key_labels = column_ref[first : first + block, :1]
+        key_labels = column_ref[first : first + block, :]
         widest = jnp.full((block, LANES), -1.0, jnp.float32)
         for q in queries:
-            scores = dot_t(keys, rows_ref[q * block : (q + 1) * block, :width])
-            same = key_labels == labels_ref[:1, q * block : (q + 1) * block]
-            scores = jnp.where(same, scores, -1.0)
+            scores = masked(
+                dot_t(keys, rows_ref[q * block : (q + 1) * block, :width]),
+                key_labels,
+                labels_ref[:1, q * block : (q + 1) * block],
+            )
             own[q] = jnp.maximum(own[q], jnp.max(scores, axis=0, keepdims=True))
             widest = widen(widest, scores)
         gained[k % (BLOCKS // 2)] = across(widest)

time: 60.4 us -> 60.2 us (level)
  other arithmetic: 1.13 us -> 0 us
  Pallas kernels: 6.3 us -> 7.06 us
    pallas_call x1, Pallas kernels: 1.41 us -> 2.5 us  [pack(): pl.pallas_call(functools.partial(pack_kernel, members), out_shape=jax.Sha...]
    add x1 -> x0, other arithmetic: 0.81 us -> none  [pack(): packed = (spot + 2 * slots * (cluster + 1)).reshape(1, rows)]
  transfers between devices with their start and end apart: 2 -> 2, of which waited for: 0 -> 1; matrix products, arithmetic and copies ran while one was open for 0% -> 0% of each run, Pallas kernels for 5% -> 5%
where the time goes in v8:
time: 60.2 us; the launch traced here: 60 us
  blocking collectives  51 us (85%)
  Pallas kernels  7.06 us (12%)
  starting transfers between devices  1.55 us (3%)
    all_to_all x1, blocking collectives, shards(): lax.all_to_all(outgoing.reshape(devices, CAP, width + LANES), ('mem', 'gr...  38.1 us
    all_to_all x1, blocking collectives, shards(): lax.all_to_all(table.reshape(devices, 1, LANES), ('mem', 'grp'), split_ax...  12.9 us
    pallas_call x1, Pallas kernels, pack(): pl.pallas_call(functools.partial(pack_kernel, members), out_shape=jax.Sha...  2.5 us
    pallas_call x1, Pallas kernels, own_best(): pl.pallas_call(own_kernel, out_shape=(jax.ShapeDtypeStruct((1, count), jn...  2.11 us
    ppermute x2, starting transfers between devices, shards(): lax.ppermute(arrived[first:first + half], 'mem', swap_cores(members))  1.55 us
  transfers between devices with their start and end apart: 2, of which 1 were waited for; matrix products, arithmetic and copies ran while one was open for 0% of the time, Pallas kernels for 5%

profile of v8, /device:TPU:1, one launch (start us, length us, event | category | flops | bytes accessed | tf_op | source)
XLA Modules:
  0.0 60.0 jit_solution(6468438543145809816)
XLA Ops:
  0.0 2.5 %shard_map.37 = bf16[1024,896]{1,0:T(8,128)(2,1)S(1)} custom-call(bf16[512,768]{1,0:T(8,128)(2,1)} %embeds_hbm.1, s32[1,512]{1,0:T(1,128)} %bitcast.21, s32[1,512]{1,0:T(1,128)} %bitcast.19), custom_call_target="tpu_custom_call" | custom-call | tf_op jit(solution)/shard_map/pallas_call | solution.py:114
  2.5 38.1 %all_to_all.10 = bf16[128,8,896]{2,1,0:T(8,128)(2,1)S(1)} all-to-all(bf16[128,8,896]{2,1,0:T(8,128)(2,1)S(1)} %bitcast.16), channel_id=1, replica_groups=mesh['grp'=16,'mem'=8] {'mem','grp'}, dimensions={0} | all-to-all | bytes 3670016 | tf_op jit(solution)/shard_map/all_to_all | solution.py:399
  40.6 0.1 slice_bitcast_fusion
  40.7 1.5 %collective-permute-start = (bf16[512,896]{1,0:T(8,128)(2,1)S(1)}, bf16[512,896]{1,0:T(8,128)(2,1)S(1)}, u32[]{:S(2)}, u32[]{:S(2)}) collective-permute-start(bf16[512,896]{1,0:T(8,128)(2,1)S(1)} %get-tuple-element.14), channel_id=1, source_target_pairs={{0,1},{1,0},{2,3},{3,2},{4,5},{5,4},{6,7},{7,6},{8,9},{9,8},{10,11... | collective-permute-start | bytes 2752520 | tf_op jit(solution)/shard_map/ppermute | solution.py:408
  42.2 0.1 collective-permute-start.1
  42.3 2.1 %shard_map.38 = (f32[1,1152]{1,0:T(1,128)S(1)}, f32[8,1152]{1,0:T(8,128)S(1)}) custom-call(bf16[1024,896]{1,0:T(8,128)(2,1)S(1)} %bitcast.13), custom_call_target="tpu_custom_call" | custom-call | tf_op jit(solution)/shard_map/pallas_call | solution.py:236
  44.4 0.0 collective-permute-done.other_ref
  44.4 0.9 %shard_map.39 = (f32[1,1152]{1,0:T(1,128)S(1)}, f32[1,512]{1,0:T(1,128)S(1)}) custom-call(f32[1,1152]{1,0:T(1,128)S(1)} %get-tuple-element.9.best_ref, f32[8,1152]{1,0:T(8,128)S(1)} %get-tuple-element.10.labels_ref, bf16[1024,896]{1,0:T(8,128)(2,1)S(1)} %bitcast.14, bf16[512,896]{1,0:T(8,128)(2,1)S(1)} %collective-permute-done.other_ref), custom_call_target="tpu_custom_call" | custom-call | tf_op jit(solution)/shard_map/pallas_call | solution.py:340
  45.3 0.0 copy-start
  45.4 0.2 collective-permute-done.1.other_ref
  45.6 0.6 shard_map.40
  46.2 12.9 %all_to_all.11 = f32[128,1,128]{2,1,0:T(1,128)S(1)} all-to-all(f32[128,1,128]{2,1,0:T(1,128)S(1)} %bitcast.17), channel_id=1, replica_groups=mesh['grp'=16,'mem'=8] {'mem','grp'}, dimensions={0} | all-to-all | bytes 131072 | tf_op jit(solution)/shard_map/all_to_all | solution.py:413
  59.1 0.0 copy-done
  59.1 0.9 %shard_map.41 = f32[1,512]{1,0:T(1,128)} custom-call(f32[128,128]{1,0:T(8,128)S(1)} %bitcast.18, s32[1,512]{1,0:T(1,128)S(1)} %bitcast.20), custom_call_target="tpu_custom_call" | custom-call | tf_op jit(solution)/shard_map/pallas_call | solution.py:386
Async XLA Ops:
  40.7 3.7 %collective-permute-start = (bf16[512,896]{1,0:T(8,128)(2,1)S(1)}, bf16[512,896]{1,0:T(8,128)(2,1)S(1)}, u32[]{:S(2)}, u32[]{:S(2)}) collective-permute-start(bf16[512,896]{1,0:T(8,128)(2,1)S(1)} %get-tuple-element.14), channel_id=1, source_target_pairs={{0,1},{1,0},{2,3},{3,2},{4,5},{5,4},{6,7},{7,6},{8,9},{9,8},{10,11... | collective-permute-start | bytes 2752520 | tf_op jit(solution)/shard_map/ppermute | solution.py:408
  42.2 3.4 %collective-permute-start.1 = (bf16[512,896]{1,0:T(8,128)(2,1)S(1)}, bf16[512,896]{1,0:T(8,128)(2,1)S(1)}, u32[]{:S(2)}, u32[]{:S(2)}) collective-permute-start(bf16[512,896]{1,0:T(8,128)(2,1)S(1)} %get-tuple-element.13), channel_id=1, source_target_pairs={{0,1},{1,0},{2,3},{3,2},{4,5},{5,4},{6,7},{7,6},{8,9},{9,8},{10,11... | collective-permute-start | bytes 2752520 | tf_op jit(solution)/shard_map/ppermute | solution.py:408
  45.3 13.7 %copy-start = (s32[512]{0:T(512)S(1)}, s32[512]{0:T(512)}, u32[]{:S(2)}) copy-start(s32[512]{0:T(512)} %param.5) | copy-start | bytes 6148

commit v9 on v8

--- a/solution.py
+++ b/solution.py
@@ -12,6 +12,7 @@
 KEPT = CAP - SHARED
 SPLIT = KEPT // 2
 LANES = 128
+OTHERS = 2 * CAP
 VMEM_LIMIT = 48 * 1024 * 1024
 
 
@@ -57,6 +58,10 @@
 
 def ones_where(mask):
     return jnp.where(mask, 1.0, 0.0).astype(jnp.bfloat16)
+
+
+def label_lines(lane, label):
+    return jnp.where(iota((LANES, lane.shape[1]), 0) == lane, label, 0.0).astype(jnp.bfloat16)
 
 
 def pack_kernel(
@@ -84,8 +89,10 @@
     here = iota((devices, rows), 0) == device
     pick_ninth = ones_where(here & (row == CAP))
     label = (cluster_ref[...] + 1).astype(jnp.float32)
-    marks = jnp.where(iota((LANES, rows), 0) == row, label, 0.0).astype(jnp.bfloat16)
-    labels = dot_t(ones_where(here), marks)
+    labels = dot_t(ones_where(here), label_lines(row, label))
+    other = (member ^ 1) * (devices // members) + group
+    here_other = ones_where(iota((devices, rows), 0) == other)
+    labels += dot_t(here_other, label_lines(row + OTHERS, label))
     for piece in range(width // LANES, CAP):
         last_ref[pl.ds(piece, devices, stride=CAP), :] = labels
 
@@ -131,19 +138,18 @@
     return CAP * ((group + 1) % (LANES // CAP)) + member
 
 
-def spread_labels(labels, slots):
-    row = iota((slots, LANES), 0)
-    lane = iota((slots, LANES), 1)
-    repeat = ones_where(iota((slots, len(labels)), 0) // CAP == iota((slots, len(labels)), 1))
-    return jnp.where(lane == row % CAP, dot(repeat, labels), 0.0).astype(
-        jnp.bfloat16
-    )
+def repeat_lines(labels, slots):
+    shape = (slots, labels.shape[0])
+    return dot(ones_where(iota(shape, 0) // CAP == iota(shape, 1)), labels)
+
+
+def only_own(lines, first):
+    own = iota(lines.shape, 1) == first + iota(lines.shape, 0) % CAP
+    return jnp.where(own, lines, 0.0)
 
 
 def in_every_lane(spots):
-    return jnp.broadcast_to(
-        jnp.sum(spots.astype(jnp.float32), axis=1, keepdims=True), spots.shape
-    )
+    return jnp.broadcast_to(jnp.sum(spots, axis=1, keepdims=True), spots.shape)
 
 
 def masked(scores, key_labels, query_labels, skip=False):
@@ -173,7 +179,9 @@
     )
 
 
-def own_kernel(rows_ref, best_ref, labels_ref, last_ref, ninth_ref, column_ref):
+def own_kernel(
+    rows_ref, best_ref, labels_ref, others_ref, last_ref, ninth_ref, column_ref
+):
     slots, wide = rows_ref.shape
     width = wide - LANES
     sources = slots // CAP
@@ -183,7 +191,9 @@
             pl.ds(piece, sources, stride=CAP), :
         ].astype(jnp.bfloat16)
     labels = last_ref[pl.ds(width // LANES, sources, stride=CAP), :].astype(jnp.bfloat16)
-    spots = spread_labels(labels, slots)
+    lines = repeat_lines(labels, slots)
+    spots = only_own(lines, 0)
+    others_ref[...] = in_every_lane(only_own(lines, OTHERS))
     groups = LANES // CAP
     source = iota((sources, LANES), 1)
     order = ones_where(
@@ -197,7 +207,7 @@
     column_ref[slots:, :] = dot(labels, at_ninth)
     at_ninth = ones_where(iota((CAP, LANES), 1) == CAP)
     row_labels = jnp.concatenate(
-        [dot_t(ones[:CAP], spots), dot_t(at_ninth, labels)], axis=1
+        [dot_t(ones[:CAP], spots.astype(jnp.bfloat16)), dot_t(at_ninth, labels)], axis=1
     )
     labels_ref[...] = row_labels
 
@@ -238,6 +248,7 @@
         out_shape=(
             jax.ShapeDtypeStruct((1, count), jnp.float32),
             jax.ShapeDtypeStruct((CAP, count), jnp.float32),
+            jax.ShapeDtypeStruct((slots, LANES), jnp.float32),
         ),
         scratch_shapes=[
             pltpu.VMEM((slots, LANES), jnp.float32),
@@ -262,21 +273,16 @@
         pl.when(jnp.logical_not(alone) & (core == index))(functools.partial(run, plan))
 
 
-def meet(plan, best_ref, labels_ref, rows_ref, other_ref, last_ref, column_ref):
-    slots, wide = rows_ref.shape
-    width = wide - LANES
+def meet(plan, best_ref, labels_ref, others_ref, rows_ref, other_ref):
+    slots = rows_ref.shape[0]
+    half, width = other_ref.shape
     block = slots // BLOCKS
-    half = other_ref.shape[0]
-    if plan:
-        last_ref[...] = other_ref[:, width:].astype(jnp.float32)
-        labels = last_ref[pl.ds(width // LANES, half // CAP, stride=CAP), :].astype(jnp.bfloat16)
-        column_ref[...] = in_every_lane(spread_labels(labels, half))
     own = [best_ref[:, q * block : (q + 1) * block] for q in range(BLOCKS)]
     gained = [jnp.full((1, block), -1.0, jnp.float32)] * (BLOCKS // 2)
     for k, queries in plan.items():
         first = k * block % half
-        keys = other_ref[first : first + block, :width]
-        key_labels = column_ref[first : first + block, :]
+        keys = other_ref[first : first + block, :]
+        key_labels = others_ref[k * block : (k + 1) * block, :]
         widest = jnp.full((block, LANES), -1.0, jnp.float32)
         for q in queries:
             scores = masked(
@@ -291,14 +297,12 @@
 
 
 def first_kernel(
-    best_ref, labels_ref, rows_ref, other_ref, out_ref, gained_ref, last_ref, column_ref
+    best_ref, labels_ref, others_ref, rows_ref, other_ref, out_ref, gained_ref
 ):
     slots = rows_ref.shape[0]
 
     def run(plan):
-        own, gained = meet(
-            plan, best_ref, labels_ref, rows_ref, other_ref, last_ref, column_ref
-        )
+        own, gained = meet(plan, best_ref, labels_ref, others_ref, rows_ref, other_ref)
         out_ref[:, :slots] = own
         out_ref[:, slots:] = best_ref[:, slots:]
         gained_ref[...] = gained
@@ -307,16 +311,14 @@
 
 
 def second_kernel(
-    best_ref, gained_ref, labels_ref, rows_ref, other_ref, out_ref, last_ref, column_ref
+    best_ref, gained_ref, labels_ref, others_ref, rows_ref, other_ref, out_ref
 ):
     slots = rows_ref.shape[0]
     groups = LANES // CAP
     shape = (groups, LANES)
 
     def run(plan):
-        own, gained = meet(
-            plan, best_ref, labels_ref, rows_ref, other_ref, last_ref, column_ref
-        )
+        own, gained = meet(plan, best_ref, labels_ref, others_ref, rows_ref, other_ref)
         gained = jnp.concatenate([gained_ref[...], gained], axis=1)
         window = iota(shape, 1) // CAP
         mine = iota(shape, 0)
@@ -333,25 +335,22 @@
     on_each_core(run, SECOND)
 
 
-def cross_best(best, labels, arrived, others):
+def cross_best(best, labels, other_labels, arrived, others):
     slots = arrived.shape[0]
     half = slots // 2
-    scratch = [pltpu.VMEM((half, LANES), jnp.float32)] * 2
     best, gained = pl.pallas_call(
         first_kernel,
         out_shape=(
             jax.ShapeDtypeStruct(best.shape, jnp.float32),
             jax.ShapeDtypeStruct((1, half), jnp.float32),
         ),
-        scratch_shapes=scratch,
         compiler_params=params(),
-    )(best, labels, arrived, others[0])
+    )(best, labels, other_labels, arrived, others[0])
     return pl.pallas_call(
         second_kernel,
         out_shape=jax.ShapeDtypeStruct((slots // CAP, LANES), jnp.float32),
-        scratch_shapes=scratch,
         compiler_params=params(),
-    )(best, gained, labels, arrived, others[1])
+    )(best, gained, labels, other_labels, arrived, others[1])
 
 
 def lookup_kernel(members, table_ref, dest_ref, out_ref):
@@ -405,11 +404,11 @@
     ).reshape(slots, width + LANES)
     half = slots // 2
     others = [
-        lax.ppermute(arrived[first : first + half], "mem", swap_cores(members))
+        lax.ppermute(arrived[first : first + half, :width], "mem", swap_cores(members))
         for first in (0, half)
     ]
-    best, labels = own_best(arrived)
-    table = cross_best(best, labels, arrived, others)
+    best, labels, other_labels = own_best(arrived)
+    table = cross_best(best, labels, other_labels, arrived, others)
     returned = lax.all_to_all(
         table.reshape(devices, 1, LANES),
         ("mem", "grp"),

time: 60.2 us -> 60 us (level)
  transfers between devices with their start and end apart: 2 -> 2, of which waited for: 1 -> 0; matrix products, arithmetic and copies ran while one was open for 0% -> 0% of each run, Pallas kernels for 5% -> 5%
where the time goes in v9:
time: 60 us; the launch traced here: 59.8 us
  blocking collectives  51 us (85%)
  Pallas kernels  7.09 us (12%)
  starting transfers between devices  1.55 us (3%)
    all_to_all x1, blocking collectives, shards(): lax.all_to_all(outgoing.reshape(devices, CAP, width + LANES), ('mem', 'gr...  38.1 us
    all_to_all x1, blocking collectives, shards(): lax.all_to_all(table.reshape(devices, 1, LANES), ('mem', 'grp'), split_ax...  13 us
    pallas_call x1, Pallas kernels, pack(): pl.pallas_call(functools.partial(pack_kernel, members), out_shape=jax.Sha...  2.5 us
    pallas_call x1, Pallas kernels, own_best(): pl.pallas_call(own_kernel, out_shape=(jax.ShapeDtypeStruct((1, count), jn...  2.14 us
    ppermute x2, starting transfers between devices, shards(): lax.ppermute(arrived[first:first + half, :width], 'mem', swap_cores(membe...  1.55 us
  transfers between devices with their start and end apart: 2, of which 0 were waited for; matrix products, arithmetic and copies ran while one was open for 0% of the time, Pallas kernels for 5%

profile of v9, /device:TPU:1, one launch (start us, length us, event | category | flops | bytes accessed | tf_op | source)
XLA Modules:
  0.0 59.8 jit_solution(2745191480643784446)
XLA Ops:
  0.0 2.5 %shard_map.37 = bf16[1024,896]{1,0:T(8,128)(2,1)S(1)} custom-call(bf16[512,768]{1,0:T(8,128)(2,1)} %embeds_hbm.1, s32[1,512]{1,0:T(1,128)} %bitcast.18, s32[1,512]{1,0:T(1,128)} %bitcast.16), custom_call_target="tpu_custom_call" | custom-call | tf_op jit(solution)/shard_map/pallas_call | solution.py:121
  2.5 38.1 %all_to_all.10 = bf16[128,8,896]{2,1,0:T(8,128)(2,1)S(1)} all-to-all(bf16[128,8,896]{2,1,0:T(8,128)(2,1)S(1)} %bitcast.13), channel_id=1, replica_groups=mesh['grp'=16,'mem'=8] {'mem','grp'}, dimensions={0} | all-to-all | bytes 3670016 | tf_op jit(solution)/shard_map/all_to_all | solution.py:398
  40.6 0.1 fusion
  40.7 1.5 %collective-permute-start = (bf16[512,768]{1,0:T(8,128)(2,1)S(1)}, bf16[512,768]{1,0:T(8,128)(2,1)S(1)}, u32[]{:S(2)}, u32[]{:S(2)}) collective-permute-start(bf16[512,768]{1,0:T(8,128)(2,1)S(1)} %get-tuple-element.16), channel_id=1, source_target_pairs={{0,1},{1,0},{2,3},{3,2},{4,5},{5,4},{6,7},{7,6},{8,9},{9,8},{10,11... | collective-permute-start | bytes 2359304 | tf_op jit(solution)/shard_map/ppermute | solution.py:407
  42.1 0.1 collective-permute-start.1
  42.2 2.1 %shard_map.38 = (f32[1,1152]{1,0:T(1,128)S(1)}, f32[8,1152]{1,0:T(8,128)S(1)}, f32[1024,128]{1,0:T(8,128)S(1)}) custom-call(bf16[1024,896]{1,0:T(8,128)(2,1)S(1)} %bitcast.10), custom_call_target="tpu_custom_call" | custom-call | tf_op jit(solution)/shard_map/pallas_call | solution.py:246
  44.4 0.0 collective-permute-done.other_ref
  44.4 0.9 %shard_map.39 = (f32[1,1152]{1,0:T(1,128)S(1)}, f32[1,512]{1,0:T(1,128)S(1)}) custom-call(f32[1,1152]{1,0:T(1,128)S(1)} %get-tuple-element.10.best_ref, f32[8,1152]{1,0:T(8,128)S(1)} %get-tuple-element.11.labels_ref, f32[1024,128]{1,0:T(8,128)S(1)} %get-tuple-element.12.others_ref, bf16[1024,896]{1,0:T(8,128)(2,1)S(1)} %bitcast.11, ...), custom_call_target="tpu_custom_call" | custom-call | tf_op jit(solution)/shard_map/pallas_call | solution.py:341
  45.3 0.0 copy-start
  45.3 0.0 collective-permute-done.1.other_ref
  45.3 0.6 shard_map.40
  45.9 13.0 %all_to_all.11 = f32[128,1,128]{2,1,0:T(1,128)S(1)} all-to-all(f32[128,1,128]{2,1,0:T(1,128)S(1)} %bitcast.14), channel_id=1, replica_groups=mesh['grp'=16,'mem'=8] {'mem','grp'}, dimensions={0} | all-to-all | bytes 131072 | tf_op jit(solution)/shard_map/all_to_all | solution.py:412
  58.9 0.0 copy-done
  58.9 0.9 %shard_map.41 = f32[1,512]{1,0:T(1,128)} custom-call(f32[128,128]{1,0:T(8,128)S(1)} %bitcast.15, s32[1,512]{1,0:T(1,128)S(1)} %bitcast.17), custom_call_target="tpu_custom_call" | custom-call | tf_op jit(solution)/shard_map/pallas_call | solution.py:385
Async XLA Ops:
  40.7 3.7 %collective-permute-start = (bf16[512,768]{1,0:T(8,128)(2,1)S(1)}, bf16[512,768]{1,0:T(8,128)(2,1)S(1)}, u32[]{:S(2)}, u32[]{:S(2)}) collective-permute-start(bf16[512,768]{1,0:T(8,128)(2,1)S(1)} %get-tuple-element.16), channel_id=1, source_target_pairs={{0,1},{1,0},{2,3},{3,2},{4,5},{5,4},{6,7},{7,6},{8,9},{9,8},{10,11... | collective-permute-start | bytes 2359304 | tf_op jit(solution)/shard_map/ppermute | solution.py:407
  42.1 3.2 %collective-permute-start.1 = (bf16[512,768]{1,0:T(8,128)(2,1)S(1)}, bf16[512,768]{1,0:T(8,128)(2,1)S(1)}, u32[]{:S(2)}, u32[]{:S(2)}) collective-permute-start(bf16[512,768]{1,0:T(8,128)(2,1)S(1)} %get-tuple-element.15), channel_id=1, source_target_pairs={{0,1},{1,0},{2,3},{3,2},{4,5},{5,4},{6,7},{7,6},{8,9},{9,8},{10,11... | collective-permute-start | bytes 2359304 | tf_op jit(solution)/shard_map/ppermute | solution.py:407
  45.3 13.6 %copy-start = (s32[512]{0:T(512)S(1)}, s32[512]{0:T(512)}, u32[]{:S(2)}) copy-start(s32[512]{0:T(512)} %param.5) | copy-start | bytes 6148

commit v10 on v9

--- a/solution.py
+++ b/solution.py
@@ -185,59 +185,71 @@
     slots, wide = rows_ref.shape
     width = wide - LANES
     sources = slots // CAP
-    last_ref[...] = rows_ref[:, width:].astype(jnp.float32)
-    for piece in range(width // LANES):
-        ninth_ref[:, piece * LANES : (piece + 1) * LANES] = last_ref[
-            pl.ds(piece, sources, stride=CAP), :
-        ].astype(jnp.bfloat16)
-    labels = last_ref[pl.ds(width // LANES, sources, stride=CAP), :].astype(jnp.bfloat16)
-    lines = repeat_lines(labels, slots)
-    spots = only_own(lines, 0)
-    others_ref[...] = in_every_lane(only_own(lines, OTHERS))
-    groups = LANES // CAP
-    source = iota((sources, LANES), 1)
-    order = ones_where(
-        iota((sources, LANES), 0) == ninth_lane(source % groups, source // groups)
-    )
-    ninth_ref[...] = dot(order, ninth_ref[...]).astype(jnp.bfloat16)
-    labels = dot(order, labels).astype(jnp.bfloat16)
-    ones = jnp.ones((LANES, LANES), jnp.bfloat16)
-    column_ref[:slots, :] = in_every_lane(spots)
-    at_ninth = ones_where(iota((LANES, LANES), 0) == CAP)
-    column_ref[slots:, :] = dot(labels, at_ninth)
-    at_ninth = ones_where(iota((CAP, LANES), 1) == CAP)
-    row_labels = jnp.concatenate(
-        [dot_t(ones[:CAP], spots.astype(jnp.bfloat16)), dot_t(at_ninth, labels)], axis=1
-    )
-    labels_ref[...] = row_labels
-
-    block = 256
-    starts = list(range(0, slots, block)) + [slots]
-    sizes = [block] * (slots // block) + [sources]
-
-    def read(i):
-        if starts[i] == slots:
-            return ninth_ref[...]
-        return rows_ref[starts[i] : starts[i] + block, :width]
-
-    best = [jnp.full((1, size), -1.0, jnp.float32) for size in sizes]
-    for k, (key, count) in enumerate(zip(starts, sizes)):
-        widest = jnp.full((count, LANES), -1.0, jnp.float32)
-        keys = read(k)
-        for q in range(k, len(starts)):
-            query, size = starts[q], sizes[q]
-            scores = masked(
-                dot_t(keys, read(q)),
-                column_ref[key : key + count, :],
-                row_labels[:1, query : query + size],
-                q == k,
+    def run(with_ninth):
+        last_ref[...] = rows_ref[:, width:].astype(jnp.float32)
+        if with_ninth:
+            for piece in range(width // LANES):
+                ninth_ref[:, piece * LANES : (piece + 1) * LANES] = last_ref[
+                    pl.ds(piece, sources, stride=CAP), :
+                ].astype(jnp.bfloat16)
+        labels = last_ref[pl.ds(width // LANES, sources, stride=CAP), :].astype(jnp.bfloat16)
+        lines = repeat_lines(labels, slots)
+        spots = only_own(lines, 0)
+        others_ref[...] = in_every_lane(only_own(lines, OTHERS))
+        if with_ninth:
+            groups = LANES // CAP
+            source = iota((sources, LANES), 1)
+            order = ones_where(
+                iota((sources, LANES), 0) == ninth_lane(source % groups, source // groups)
             )
-            best[q] = jnp.maximum(best[q], jnp.max(scores, axis=0, keepdims=True))
-            if q > k:
-                widest = widen(widest, scores)
-        if k + 1 < len(starts):
-            best[k] = jnp.maximum(best[k], across(widest))
-        best_ref[:, key : key + count] = best[k]
+            ninth_ref[...] = dot(order, ninth_ref[...]).astype(jnp.bfloat16)
+            labels = dot(order, labels).astype(jnp.bfloat16)
+        ones = jnp.ones((LANES, LANES), jnp.bfloat16)
+        column_ref[:slots, :] = in_every_lane(spots)
+        at_ninth = ones_where(iota((LANES, LANES), 0) == CAP)
+        column_ref[slots:, :] = dot(labels, at_ninth)
+        at_ninth = ones_where(iota((CAP, LANES), 1) == CAP)
+        row_labels = jnp.concatenate(
+            [dot_t(ones[:CAP], spots.astype(jnp.bfloat16)), dot_t(at_ninth, labels)], axis=1
+        )
+        labels_ref[...] = row_labels
+
+        block = 256
+        starts = list(range(0, slots, block))
+        sizes = [block] * len(starts)
+        if with_ninth:
+            starts.append(slots)
+            sizes.append(sources)
+        else:
+            best_ref[:, slots:] = jnp.full((1, sources), -1.0, jnp.float32)
+
+        def read(i):
+            if starts[i] == slots:
+                return ninth_ref[...]
+            return rows_ref[starts[i] : starts[i] + block, :width]
+
+        best = [jnp.full((1, size), -1.0, jnp.float32) for size in sizes]
+        for k, (key, count) in enumerate(zip(starts, sizes)):
+            widest = jnp.full((count, LANES), -1.0, jnp.float32)
+            keys = read(k)
+            for q in range(k, len(starts)):
+                query, size = starts[q], sizes[q]
+                scores = masked(
+                    dot_t(keys, read(q)),
+                    column_ref[key : key + count, :],
+                    row_labels[:1, query : query + size],
+                    q == k,
+                )
+                best[q] = jnp.maximum(best[q], jnp.max(scores, axis=0, keepdims=True))
+                if q > k:
+                    widest = widen(widest, scores)
+            if k + 1 < len(starts):
+                best[k] = jnp.maximum(best[k], across(widest))
+            best_ref[:, key : key + count] = best[k]
+
+    spread = lax.axis_index("mem") < 2
+    pl.when(spread)(lambda: run(False))
+    pl.when(jnp.logical_not(spread))(lambda: run(True))
 
 
 def own_best(arrived):

time: 60 us -> 60 us (level)
  transfers between devices with their start and end apart: 2 -> 2, of which waited for: 0 -> 2; matrix products, arithmetic and copies ran while one was open for 0% -> 0% of each run, Pallas kernels for 5% -> 4%
where the time goes in v10:
time: 60 us; the launch traced here: 59.8 us
  blocking collectives  51.2 us (85%)
  Pallas kernels  6.52 us (11%)
  starting transfers between devices  1.55 us (3%)
    all_to_all x1, blocking collectives, shards(): lax.all_to_all(outgoing.reshape(devices, CAP, width + LANES), ('mem', 'gr...  38.1 us
    all_to_all x1, blocking collectives, shards(): lax.all_to_all(table.reshape(devices, 1, LANES), ('mem', 'grp'), split_ax...  13.2 us
    pallas_call x1, Pallas kernels, pack(): pl.pallas_call(functools.partial(pack_kernel, members), out_shape=jax.Sha...  2.5 us
    pallas_call x1, Pallas kernels, own_best(): pl.pallas_call(own_kernel, out_shape=(jax.ShapeDtypeStruct((1, count), jn...  1.64 us
    ppermute x2, starting transfers between devices, shards(): lax.ppermute(arrived[first:first + half, :width], 'mem', swap_cores(membe...  1.55 us
  transfers between devices with their start and end apart: 2, of which 2 were waited for; matrix products, arithmetic and copies ran while one was open for 0% of the time, Pallas kernels for 4%

profile of v10, /device:TPU:1, one launch (start us, length us, event | category | flops | bytes accessed | tf_op | source)
XLA Modules:
  0.0 59.8 jit_solution(9430976731676721703)
XLA Ops:
  0.0 2.5 %shard_map.37 = bf16[1024,896]{1,0:T(8,128)(2,1)S(1)} custom-call(bf16[512,768]{1,0:T(8,128)(2,1)} %embeds_hbm.1, s32[1,512]{1,0:T(1,128)} %bitcast.18, s32[1,512]{1,0:T(1,128)} %bitcast.16), custom_call_target="tpu_custom_call" | custom-call | tf_op jit(solution)/shard_map/pallas_call | solution.py:121
  2.5 38.1 %all_to_all.10 = bf16[128,8,896]{2,1,0:T(8,128)(2,1)S(1)} all-to-all(bf16[128,8,896]{2,1,0:T(8,128)(2,1)S(1)} %bitcast.13), channel_id=1, replica_groups=mesh['grp'=16,'mem'=8] {'mem','grp'}, dimensions={0} | all-to-all | bytes 3670016 | tf_op jit(solution)/shard_map/all_to_all | solution.py:410
  40.6 0.1 fusion
  40.7 1.5 %collective-permute-start = (bf16[512,768]{1,0:T(8,128)(2,1)S(1)}, bf16[512,768]{1,0:T(8,128)(2,1)S(1)}, u32[]{:S(2)}, u32[]{:S(2)}) collective-permute-start(bf16[512,768]{1,0:T(8,128)(2,1)S(1)} %get-tuple-element.16), channel_id=1, source_target_pairs={{0,1},{1,0},{2,3},{3,2},{4,5},{5,4},{6,7},{7,6},{8,9},{9,8},{10,11... | collective-permute-start | bytes 2359304 | tf_op jit(solution)/shard_map/ppermute | solution.py:419
  42.1 0.1 collective-permute-start.1
  42.2 1.6 %shard_map.38 = (f32[1,1152]{1,0:T(1,128)S(1)}, f32[8,1152]{1,0:T(8,128)S(1)}, f32[1024,128]{1,0:T(8,128)S(1)}) custom-call(bf16[1024,896]{1,0:T(8,128)(2,1)S(1)} %bitcast.10), custom_call_target="tpu_custom_call" | custom-call | tf_op jit(solution)/shard_map/pallas_call | solution.py:258
  43.9 0.2 collective-permute-done.other_ref
  44.1 0.9 %shard_map.39 = (f32[1,1152]{1,0:T(1,128)S(1)}, f32[1,512]{1,0:T(1,128)S(1)}) custom-call(f32[1,1152]{1,0:T(1,128)S(1)} %get-tuple-element.10.best_ref, f32[8,1152]{1,0:T(8,128)S(1)} %get-tuple-element.11.labels_ref, f32[1024,128]{1,0:T(8,128)S(1)} %get-tuple-element.12.others_ref, bf16[1024,896]{1,0:T(8,128)(2,1)S(1)} %bitcast.11, ...), custom_call_target="tpu_custom_call" | custom-call | tf_op jit(solution)/shard_map/pallas_call | solution.py:353
  44.9 0.0 copy-start
  45.0 0.2 collective-permute-done.1.other_ref
  45.2 0.5 shard_map.40
  45.7 13.2 %all_to_all.11 = f32[128,1,128]{2,1,0:T(1,128)S(1)} all-to-all(f32[128,1,128]{2,1,0:T(1,128)S(1)} %bitcast.14), channel_id=1, replica_groups=mesh['grp'=16,'mem'=8] {'mem','grp'}, dimensions={0} | all-to-all | bytes 131072 | tf_op jit(solution)/shard_map/all_to_all | solution.py:424
  58.9 0.0 copy-done
  58.9 0.9 %shard_map.41 = f32[1,512]{1,0:T(1,128)} custom-call(f32[128,128]{1,0:T(8,128)S(1)} %bitcast.15, s32[1,512]{1,0:T(1,128)S(1)} %bitcast.17), custom_call_target="tpu_custom_call" | custom-call | tf_op jit(solution)/shard_map/pallas_call | solution.py:397
Async XLA Ops:
  40.7 3.4 %collective-permute-start = (bf16[512,768]{1,0:T(8,128)(2,1)S(1)}, bf16[512,768]{1,0:T(8,128)(2,1)S(1)}, u32[]{:S(2)}, u32[]{:S(2)}) collective-permute-start(bf16[512,768]{1,0:T(8,128)(2,1)S(1)} %get-tuple-element.16), channel_id=1, source_target_pairs={{0,1},{1,0},{2,3},{3,2},{4,5},{5,4},{6,7},{7,6},{8,9},{9,8},{10,11... | collective-permute-start | bytes 2359304 | tf_op jit(solution)/shard_map/ppermute | solution.py:419
  42.1 3.0 %collective-permute-start.1 = (bf16[512,768]{1,0:T(8,128)(2,1)S(1)}, bf16[512,768]{1,0:T(8,128)(2,1)S(1)}, u32[]{:S(2)}, u32[]{:S(2)}) collective-permute-start(bf16[512,768]{1,0:T(8,128)(2,1)S(1)} %get-tuple-element.15), channel_id=1, source_target_pairs={{0,1},{1,0},{2,3},{3,2},{4,5},{5,4},{6,7},{7,6},{8,9},{9,8},{10,11... | collective-permute-start | bytes 2359304 | tf_op jit(solution)/shard_map/ppermute | solution.py:419
  44.9 13.9 %copy-start = (s32[512]{0:T(512)S(1)}, s32[512]{0:T(512)}, u32[]{:S(2)}) copy-start(s32[512]{0:T(512)} %param.5) | copy-start | bytes 6148

commit v11 on v9

--- a/solution.py
+++ b/solution.py
@@ -65,7 +65,7 @@
 
 
 def pack_kernel(
-    members, embeds_hbm, cluster_hbm, dest_hbm, out_ref,
+    members, embeds_hbm, cluster_hbm, dest_hbm, out_ref, device_ref, lane_ref,
     embeds_ref, cluster_ref, dest_ref, unit_ref, last_ref, sems,
 ):
     rows, width = embeds_ref.shape
@@ -88,8 +88,11 @@
     picks = [ones_where(b + iota((block, rows), 0) == slot) for b in range(0, slots, block)]
     here = iota((devices, rows), 0) == device
     pick_ninth = ones_where(here & (row == CAP))
+    device_ref[...] = ones_where(here)
+    mine, seat = lax.axis_index("grp"), lax.axis_index("mem")
+    lane_ref[...] = jnp.where(row < CAP, CAP * mine + row, ninth_lane(mine, seat))
     label = (cluster_ref[...] + 1).astype(jnp.float32)
-    labels = dot_t(ones_where(here), label_lines(row, label))
+    labels = dot_t(device_ref[...], label_lines(row, label))
     other = (member ^ 1) * (devices // members) + group
     here_other = ones_where(iota((devices, rows), 0) == other)
     labels += dot_t(here_other, label_lines(row + OTHERS, label))
@@ -120,7 +123,11 @@
     ]
     return pl.pallas_call(
         functools.partial(pack_kernel, members),
-        out_shape=jax.ShapeDtypeStruct((slots, width + LANES), jnp.bfloat16),
+        out_shape=(
+            jax.ShapeDtypeStruct((slots, width + LANES), jnp.bfloat16),
+            jax.ShapeDtypeStruct((slots // CAP, rows), jnp.bfloat16),
+            jax.ShapeDtypeStruct((1, rows), jnp.int32),
+        ),
         in_specs=[pl.BlockSpec(memory_space=pltpu.HBM)] * 3,
         scratch_shapes=[
             pltpu.VMEM((rows, width), jnp.bfloat16),
@@ -353,9 +360,9 @@
     )(best, gained, labels, other_labels, arrived, others[1])
 
 
-def lookup_kernel(members, table_ref, dest_ref, out_ref):
+def lookup_kernel(members, table_ref, device_ref, lane_ref, out_ref):
     devices = table_ref.shape[0]
-    rows = dest_ref.shape[1]
+    rows = lane_ref.shape[1]
     mine = lax.axis_index("grp")
     groups = devices // members
     table = table_ref[...]
@@ -366,27 +373,25 @@
     )
     window = iota((devices, LANES), 1) // CAP
     table = jnp.where(window == mine, jnp.maximum(table, other), table)
-    group, member, row = place(dest_ref[...], members)
-    pick = ones_where(iota((devices, rows), 0) == member * groups + group)
+    pick = device_ref[...]
     parts = []
     left = table.T
     for _ in range(3):
         parts.append(left.astype(jnp.bfloat16))
         left = left - parts[-1].astype(jnp.float32)
     found = dot(jnp.concatenate(parts, axis=1), jnp.concatenate([pick] * 3, axis=0))
-    lane = jnp.where(row < CAP, CAP * mine + row, ninth_lane(mine, lax.axis_index("mem")))
     out_ref[...] = jnp.max(
-        jnp.where(iota((LANES, rows), 0) == lane, found, -1.0), axis=0, keepdims=True
-    )
-
-
-def lookup(table, dest, members):
-    rows = dest.shape[0]
+        jnp.where(iota((LANES, rows), 0) == lane_ref[...], found, -1.0), axis=0, keepdims=True
+    )
+
+
+def lookup(table, device, lane, members):
+    rows = lane.shape[1]
     return pl.pallas_call(
         functools.partial(lookup_kernel, members),
         out_shape=jax.ShapeDtypeStruct((1, rows), jnp.float32),
         compiler_params=params(),
-    )(table, dest.reshape(1, rows)).reshape(rows)
+    )(table, device, lane).reshape(rows)
 
 
 def shards(embeds, cluster, dest):
@@ -394,7 +399,7 @@
     devices = lax.axis_size("grp") * members
     width = embeds.shape[1]
     slots = devices * CAP
-    outgoing = pack(embeds, cluster, dest, slots, members)
+    outgoing, device, lane = pack(embeds, cluster, dest, slots, members)
     arrived = lax.all_to_all(
         outgoing.reshape(devices, CAP, width + LANES),
         ("mem", "grp"),
@@ -416,7 +421,7 @@
         concat_axis=0,
         tiled=True,
     ).reshape(devices, LANES)
-    return lookup(returned, dest, members)
+    return lookup(returned, device, lane, members)
 
 
 def solution(mesh):

time: 60 us -> 60 us (level)
  no operation moved by 1% of the time
where the time goes in v11:
time: 60 us; the launch traced here: 59.8 us
  blocking collectives  51 us (85%)
  Pallas kernels  7.08 us (12%)
  starting transfers between devices  1.55 us (3%)
    all_to_all x1, blocking collectives, shards(): lax.all_to_all(outgoing.reshape(devices, CAP, width + LANES), ('mem', 'gr...  38.1 us
    all_to_all x1, blocking collectives, shards(): lax.all_to_all(table.reshape(devices, 1, LANES), ('mem', 'grp'), split_ax...  13 us
    pallas_call x1, Pallas kernels, pack(): pl.pallas_call(functools.partial(pack_kernel, members), out_shape=(jax.Sh...  2.5 us
    pallas_call x1, Pallas kernels, own_best(): pl.pallas_call(own_kernel, out_shape=(jax.ShapeDtypeStruct((1, count), jn...  2.14 us
    ppermute x2, starting transfers between devices, shards(): lax.ppermute(arrived[first:first + half, :width], 'mem', swap_cores(membe...  1.55 us
  transfers between devices with their start and end apart: 2, of which 0 were waited for; matrix products, arithmetic and copies ran while one was open for 0% of the time, Pallas kernels for 5%

profile of v11, /device:TPU:1, one launch (start us, length us, event | category | flops | bytes accessed | tf_op | source)
XLA Modules:
  0.0 59.8 jit_solution(1085238600319788142)
XLA Ops:
  0.0 2.5 %shard_map.37 = (bf16[1024,896]{1,0:T(8,128)(2,1)S(1)}, bf16[128,512]{1,0:T(8,128)(2,1)S(1)}, s32[1,512]{1,0:T(1,128)S(1)}) custom-call(bf16[512,768]{1,0:T(8,128)(2,1)} %embeds_hbm.1, s32[1,512]{1,0:T(1,128)} %bitcast.16, s32[1,512]{1,0:T(1,128)} %bitcast.17), custom_call_target="tpu_custom_call" | custom-call | tf_op jit(solution)/shard_map/pallas_call | solution.py:124
  2.5 38.1 %all_to_all.10 = bf16[128,8,896]{2,1,0:T(8,128)(2,1)S(1)} all-to-all(bf16[128,8,896]{2,1,0:T(8,128)(2,1)S(1)} %bitcast.13), channel_id=1, replica_groups=mesh['grp'=16,'mem'=8] {'mem','grp'}, dimensions={0} | all-to-all | bytes 3670016 | tf_op jit(solution)/shard_map/all_to_all | solution.py:403
  40.6 0.1 fusion
  40.7 1.5 %collective-permute-start = (bf16[512,768]{1,0:T(8,128)(2,1)S(1)}, bf16[512,768]{1,0:T(8,128)(2,1)S(1)}, u32[]{:S(2)}, u32[]{:S(2)}) collective-permute-start(bf16[512,768]{1,0:T(8,128)(2,1)S(1)} %get-tuple-element.22), channel_id=1, source_target_pairs={{0,1},{1,0},{2,3},{3,2},{4,5},{5,4},{6,7},{7,6},{8,9},{9,8},{10,11... | collective-permute-start | bytes 2359304 | tf_op jit(solution)/shard_map/ppermute | solution.py:412
  42.1 0.1 collective-permute-start.1
  42.2 2.1 %shard_map.38 = (f32[1,1152]{1,0:T(1,128)S(1)}, f32[8,1152]{1,0:T(8,128)S(1)}, f32[1024,128]{1,0:T(8,128)S(1)}) custom-call(bf16[1024,896]{1,0:T(8,128)(2,1)S(1)} %bitcast.10), custom_call_target="tpu_custom_call" | custom-call | tf_op jit(solution)/shard_map/pallas_call | solution.py:253
  44.4 0.0 collective-permute-done.other_ref
  44.4 0.9 %shard_map.39 = (f32[1,1152]{1,0:T(1,128)S(1)}, f32[1,512]{1,0:T(1,128)S(1)}) custom-call(f32[1,1152]{1,0:T(1,128)S(1)} %get-tuple-element.14.best_ref, f32[8,1152]{1,0:T(8,128)S(1)} %get-tuple-element.15.labels_ref, f32[1024,128]{1,0:T(8,128)S(1)} %get-tuple-element.16.others_ref, bf16[1024,896]{1,0:T(8,128)(2,1)S(1)} %bitcast.11, ...), custom_call_target="tpu_custom_call" | custom-call | tf_op jit(solution)/shard_map/pallas_call | solution.py:348
  45.3 0.0 collective-permute-done.1.other_ref
  45.3 0.6 shard_map.40
  45.9 13.0 %all_to_all.11 = f32[128,1,128]{2,1,0:T(1,128)S(1)} all-to-all(f32[128,1,128]{2,1,0:T(1,128)S(1)} %bitcast.14), channel_id=1, replica_groups=mesh['grp'=16,'mem'=8] {'mem','grp'}, dimensions={0} | all-to-all | bytes 131072 | tf_op jit(solution)/shard_map/all_to_all | solution.py:417
  58.9 0.9 %shard_map.41 = f32[1,512]{1,0:T(1,128)} custom-call(f32[128,128]{1,0:T(8,128)S(1)} %bitcast.15, bf16[128,512]{1,0:T(8,128)(2,1)S(1)} %get-tuple-element.19.device_ref, s32[1,512]{1,0:T(1,128)S(1)} %get-tuple-element.20.lane_ref), custom_call_target="tpu_custom_call" | custom-call | tf_op jit(solution)/shard_map/pallas_call | solution.py:390
Async XLA Ops:
  40.7 3.7 %collective-permute-start = (bf16[512,768]{1,0:T(8,128)(2,1)S(1)}, bf16[512,768]{1,0:T(8,128)(2,1)S(1)}, u32[]{:S(2)}, u32[]{:S(2)}) collective-permute-start(bf16[512,768]{1,0:T(8,128)(2,1)S(1)} %get-tuple-element.22), channel_id=1, source_target_pairs={{0,1},{1,0},{2,3},{3,2},{4,5},{5,4},{6,7},{7,6},{8,9},{9,8},{10,11... | collective-permute-start | bytes 2359304 | tf_op jit(solution)/shard_map/ppermute | solution.py:412
  42.1 3.2 %collective-permute-start.1 = (bf16[512,768]{1,0:T(8,128)(2,1)S(1)}, bf16[512,768]{1,0:T(8,128)(2,1)S(1)}, u32[]{:S(2)}, u32[]{:S(2)}) collective-permute-start(bf16[512,768]{1,0:T(8,128)(2,1)S(1)} %get-tuple-element.21), channel_id=1, source_target_pairs={{0,1},{1,0},{2,3},{3,2},{4,5},{5,4},{6,7},{7,6},{8,9},{9,8},{10,11... | collective-permute-start | bytes 2359304 | tf_op jit(solution)/shard_map/ppermute | solution.py:412
